TPU v7x, 32 devices: a whole 2x2x4 slice. The times are simulated.
32 devices in a mesh: head: 8 (over z, core), key: 4 (over y, x).
Axes of the slice: x: 2, y: 2, z: 4, core: 2. Of those that a mesh axis runs over, the one named last changes fastest.
Arguments:
- tokens: bfloat16 [4096, 2048], P(('head', 'key')), may hold values from -6 to 6
- upstream: bfloat16 [4096, 2048], P(('head', 'key')), may hold values from -6 to 6
- route_weight: float32 [4096, 8], P(('head', 'key')), may hold values from 0.02 to 0.5
- expert_ids: int32 [4096, 8], P(('head', 'key')), may hold values from 0 to 31, all different within a row; in each aligned block of 128 rows (0 to 127, 128 to 255, ...) at most 36 rows name the same one
- w_gate_up: bfloat16 [32, 2048, 1536], P(('head', 'key')), may hold values from -0.125 to 0.125
- w_down: bfloat16 [32, 768, 2048], P(('head', 'key')), may hold values from -0.21875 to 0.21875
- w_out: bfloat16 [4096, 2048], P('head'), may hold values from -0.09375 to 0.09375
- queries: bfloat16 [128, 4096], P(None, 'head'), may hold values from -4 to 4
- keys_values: bfloat16 [4096, 1024], P('key'), may hold values from -4 to 4
- key_blocks: int32 [32], P('key'), may hold values from 0 to 31, as said below
- attn_out: bfloat16 [128, 4096], P(None, 'head'), may hold values from -5 to 5, as said below
- attn_lse: float32 [32, 128], P('head'), may hold values from -200 to 200, as said below
Outputs:
- d_resid: bfloat16 [4096, 2048], P(('head', 'key'))
- grad_gate_up: bfloat16 [32, 2048, 1536], P(('head', 'key'))
- grad_down: bfloat16 [32, 768, 2048], P(('head', 'key'))
- grad_out: bfloat16 [4096, 2048], P('head', 'key')
- d_queries: bfloat16 [128, 4096], P('key', 'head')
- d_keys_values: bfloat16 [4096, 1024], P('key', 'head')
Inputs may be any that keep to these rules, and one draw needn't show every extreme that they name: `expert_ids`: each row names 8 different experts; within one block of 128 rows no expert is named more than 36 times, and in some block one is named exactly 36 times. `key_blocks`: every block number appears once. `attn_out`: the forward attention output of these queries, keys and values under the causal rule of the steps, with probabilities rounded to bfloat16 before the product with values. `attn_lse`: the log of the sum over visible keys of exp of the scaled scores, for each head and query, as in the forward pass.
All inputs are finite; a program needn't handle non-finite values.
Results may differ from a plain program's by a relative error of at most 0.011.
Values may be sent and summed in bfloat16 or wider, within the bound.
No kernel may reach another device: no remote copies, remote signals or barrier semaphores. Data moves between devices by JAX's collectives and lax.ppermute only.
A program may use at most 192 MiB of HBM per device.

v0:
```python
import functools

import jax
import jax.numpy as jnp
from jax import lax
from jax.experimental import pallas as pl
from jax.experimental.pallas import tpu as pltpu
from jax.sharding import PartitionSpec as P

QH = 32
KVH = 4
HD = 128
KBLK = 128

BF = jnp.bfloat16
F32 = jnp.float32


def dot(a, b, contract):
    return lax.dot_general(a, b, (contract, ((), ())), preferred_element_type=F32)


HEAD = ("z", "core")


def swap(block, axis, mask):
    count = lax.axis_size(axis)
    return lax.ppermute(block, axis, [(i, i ^ mask) for i in range(count)])


def along_z(block, step):
    count = lax.axis_size(HEAD)
    route = [(i, i + 2 * step) for i in range(count) if 0 <= i + 2 * step < count]
    return lax.ppermute(block, HEAD, route)


def pick(z, options):
    out = options[-1]
    for height in range(len(options) - 2, -1, -1):
        if options[height] is not out:
            out = jnp.where(z == height, options[height], out)
    return out


def gather_z(block, z, count):
    up, down = [block], [block]
    for _ in range(count - 1):
        up.append(along_z(up[-1], 1))
        down.append(along_z(down[-1], -1))
    blocks = [block]
    for mask in range(1, count):
        options = []
        for height in range(count):
            distance = (height ^ mask) - height
            options.append(down[distance] if distance > 0 else up[-distance])
        blocks.append(pick(z, options))
    return blocks


def last_to_all(block):
    n_head = lax.axis_size(HEAD)
    n_key = lax.axis_size("key")
    axes = ("z", "core", "key")
    me = lax.axis_index(HEAD) * n_key + lax.axis_index("key")
    held = {n_head * n_key - 1}

    def send(block, move):
        route = [(i, move(i)) for i in sorted(held) if move(i) is not None]
        arrived = lax.ppermute(block, axes, route)
        takes = jnp.zeros((), jnp.bool_)
        for _, target in route:
            takes = takes | (me == target)
            held.add(target)
        return jnp.where(takes, arrived, block)

    bit = 1
    while bit < n_key:
        block = send(block, lambda i: i ^ bit)
        bit *= 2
    for height in range(n_head // 2 - 1, 0, -1):
        block = send(block, lambda i: i - 2 * n_key if i // (2 * n_key) == height else None)
    return send(block, lambda i: i ^ n_key)


def route_tables(ids, weights, first_expert, key, n_key):
    blocks, top, tokens = ids.shape
    experts = first_expert + jnp.bitwise_xor(key, jnp.arange(n_key, dtype=jnp.int32))
    hit = ids[:, None, :, :] == experts[None, :, None, None]
    chosen = jnp.any(hit, axis=2)
    weight = jnp.sum(jnp.where(hit, weights[:, None], 0.0), axis=2)
    order = jnp.arange(tokens, dtype=jnp.int32)
    before = (order[:, None] < order[None, :]).astype(BF)
    place = dot(chosen.reshape(blocks * n_key, tokens).astype(BF), before, ((1,), (0,)))
    place = place.reshape(blocks, n_key, tokens)
    return jnp.where(chosen, place, -1.0), weight


def layer_plain(tokens, upstream, route_weight, expert_ids, w_gate_up, w_down, early, attend):
    tok_dev, d_model = tokens.shape
    top_count = expert_ids.shape[1]
    n_head = lax.axis_size(HEAD)
    n_key = lax.axis_size("key")
    n_z = n_head // 2
    devices = n_head * n_key
    cap = max(2, 9 * tok_dev * top_count // (8 * devices))
    head = lax.axis_index(HEAD)
    key = lax.axis_index("key")
    z = head // 2
    core = head % 2
    hidden_width = w_down.shape[0]

    info = jnp.concatenate([expert_ids.T.astype(F32), route_weight.T], axis=0)
    info_all = lax.all_gather(info, HEAD)
    place_all, weight_all = route_tables(
        info_all[:, :top_count].astype(jnp.int32),
        info_all[:, top_count:],
        head * n_key,
        key,
        n_key,
    )

    pair_slots = 2 * cap
    dest_rows = 2 * pair_slots
    sel_rows = n_key * dest_rows
    row = jnp.arange(sel_rows, dtype=jnp.int32)
    row_mask = row // dest_rows
    row_kind = row % dest_rows // pair_slots
    row_side = row % pair_slots // cap
    row_slot = row % cap
    col = jnp.arange(4 * tok_dev, dtype=jnp.int32)
    col_side = col // (2 * tok_dev)
    col_kind = col % (2 * tok_dev) // tok_dev
    row_pick = (row_mask[:, None] == jnp.arange(n_key)[None, :]).astype(BF)
    sel_meets = (row_kind[:, None] == col_kind[None, :]) & (row_side[:, None] == col_side[None, :])

    back_rows = n_key * pair_slots
    brow = jnp.arange(back_rows, dtype=jnp.int32)
    bcol = jnp.arange(2 * tok_dev, dtype=jnp.int32)
    back_pick = (brow[:, None] // pair_slots == jnp.arange(n_key)[None, :]).astype(BF)
    back_meets = (brow % pair_slots // cap)[:, None] == (bcol // tok_dev)[None, :]
    back_slot = brow % cap

    own = jnp.concatenate([tokens, upstream], axis=0)
    chunks = gather_z(own, z, n_z)

    kept = []
    returns = []
    for mask in range(n_z):
        source = jnp.bitwise_xor(z, mask) * 2
        mine, theirs = source + core, source + 1 - core
        place = jnp.stack([place_all[mine], place_all[theirs]], axis=1)
        weight = jnp.stack([weight_all[mine], weight_all[theirs]], axis=1)
        place_cols = jnp.broadcast_to(
            place[:, :, None, :], (n_key, 2, 2, tok_dev)
        ).reshape(n_key, 4 * tok_dev)
        weight_cols = jnp.broadcast_to(
            weight[:, :, None, :], (n_key, 2, 2, tok_dev)
        ).reshape(n_key, 4 * tok_dev)
        place_at = dot(row_pick, place_cols.astype(BF), ((1,), (0,)))
        chosen = (place_at == row_slot[:, None].astype(F32)) & sel_meets
        weight_at = lax.dot_general(
            row_pick.astype(F32),
            weight_cols,
            (((1,), (0,)), ((), ())),
            precision=lax.Precision.HIGHEST,
            preferred_element_type=F32,
        )
        scale = jnp.sum(jnp.where(chosen, weight_at, 0.0), axis=1)
        scale = jnp.where(row_kind == 0, 1.0, scale)
        chunk = chunks[mask]
        both = jnp.concatenate([chunk, swap(chunk, "core", 1)], axis=0)
        selected = dot(chosen.astype(BF), both, ((1,), (0,))) * scale[:, None]
        selected = selected.astype(BF)
        pieces = [selected[m * dest_rows : (m + 1) * dest_rows] for m in range(n_key)]
        pieces = [pieces[0]] + [swap(pieces[m], "key", m) for m in range(1, n_key)]
        expert_in = jnp.concatenate([p[:pair_slots] for p in pieces], axis=0)
        scaled_in = jnp.concatenate([p[pair_slots:] for p in pieces], axis=0)

        gate_up = dot(expert_in, w_gate_up, ((1,), (0,)))
        gate = gate_up[:, :hidden_width]
        up = gate_up[:, hidden_width:]
        sigma = jax.nn.sigmoid(gate)
        activated = gate * sigma
        hidden = (activated * up).astype(BF)
        d_hidden = dot(scaled_in, w_down, ((1,), (1,)))
        d_gate = d_hidden * up * sigma * (1.0 + gate * (1.0 - sigma))
        d_up = d_hidden * activated
        d_gate_up = jnp.concatenate([d_gate, d_up], axis=1).astype(BF)
        d_rows = dot(d_gate_up, w_gate_up, ((1,), (1,))).astype(BF)
        kept.append((expert_in, scaled_in, hidden, d_gate_up))

        back = [d_rows[m * pair_slots : (m + 1) * pair_slots] for m in range(n_key)]
        back = [back[0]] + [swap(back[m], "key", m) for m in range(1, n_key)]
        back = jnp.concatenate(back, axis=0)
        back_place = place.reshape(n_key, 2 * tok_dev).astype(BF)
        back_at = dot(back_pick, back_place, ((1,), (0,)))
        back_chosen = (back_at == back_slot[:, None].astype(F32)) & back_meets
        part = dot(back_chosen.astype(BF), back, ((0,), (0,)))
        total = part[:tok_dev] + swap(part[tok_dev:].astype(BF), "core", 1).astype(F32)
        returns.append(total)

    resid = upstream.astype(F32) + returns[0]
    for mask in range(1, n_z):
        resid = resid + swap(returns[mask].astype(BF), "z", mask).astype(F32)
    d_resid = resid.astype(BF)

    expert_in, scaled_in, hidden, d_gate_up = (
        jnp.concatenate([entry[i] for entry in kept], axis=0) for i in range(4)
    )
    grad_down = dot(hidden, scaled_in, ((0,), (0,))).astype(BF)
    grad_gate_up = dot(expert_in, d_gate_up, ((0,), (0,))).astype(BF)
    return (d_resid, grad_gate_up, grad_down, *attend(last_to_all(d_resid))[0])


INFO_ROWS = 16
VMEM_LIMIT = 56 * 2**20


def params():
    return pltpu.CompilerParams(vmem_limit_bytes=VMEM_LIMIT)


def cost():
    return pl.CostEstimate(flops=1000, bytes_accessed=1000, transcendentals=0)


ANY = pl.BlockSpec(memory_space=pl.ANY)


def build_kernel(ids_ref, weight_ref, tokens_ref, out_ref):
    rows = tokens_ref.shape[0]
    out_ref[:rows] = tokens_ref[...]
    weight = weight_ref[...]
    high = weight.astype(BF).astype(F32)
    middle = (weight - high).astype(BF).astype(F32)
    low = weight - high - middle
    parts = jnp.concatenate([ids_ref[...].astype(F32), high, middle, low], axis=1)
    parts = jnp.concatenate([parts, jnp.zeros_like(parts)], axis=0)
    out_ref[rows:] = jnp.zeros((INFO_ROWS, out_ref.shape[1]), BF)
    out_ref[rows:, : parts.shape[1]] = parts.astype(BF)


def build(ids, weights, tokens):
    rows, width = tokens.shape
    return pl.pallas_call(
        build_kernel,
        out_shape=jax.ShapeDtypeStruct((rows + INFO_ROWS, width), BF),
        compiler_params=params(),
        cost_estimate=cost(),
        name="build_block",
    )(ids, weights, tokens)


def select_kernel(n_key, cap, top, rows, meta, xa, xb, ia, ib, after, out_ref, hot_out, scale_out, hot_ref):
    slots = 2 * cap

    @pl.when(pl.program_id(1) == 0)
    def _():
        order = lax.broadcasted_iota(jnp.int32, (rows, rows), 0)
        later = lax.broadcasted_iota(jnp.int32, (rows, rows), 1)
        before = jnp.where(order < later, 1.0, 0.0).astype(BF)
        places, scales = [], []
        for ref in (ia, ib):
            info = ref[...].astype(F32)[:top]
            ids = info[:, :rows]
            weight = info[:, rows : 2 * rows] + info[:, 2 * rows : 3 * rows]
            weight = weight + info[:, 3 * rows : 4 * rows]
            chosen, scale = [], []
            for m in range(n_key):
                expert = (meta[0] + m).astype(F32)
                hit = ids == expert
                chosen.append(jnp.max(jnp.where(hit, 1.0, 0.0), axis=0, keepdims=True))
                scale.append(jnp.sum(jnp.where(hit, weight, 0.0), axis=0, keepdims=True))
            chosen = jnp.concatenate(chosen, axis=0)
            place = jnp.dot(chosen.astype(BF), before, preferred_element_type=F32)
            places.append(jnp.where(chosen > 0.0, place, -1.0e6))
            scales.append(scale)
        row = lax.broadcasted_iota(jnp.int32, (n_key * slots, 2 * rows), 0).astype(F32)
        hot = jnp.zeros((n_key * slots, 2 * rows), F32)
        weighted = jnp.zeros((n_key * slots, 2 * rows), F32)
        for m in range(n_key):
            at = jnp.concatenate([places[0][m : m + 1], places[1][m : m + 1] + cap], axis=1)
            scale = jnp.concatenate([scales[0][m], scales[1][m]], axis=1)
            hit = row == at + m * slots
            hot = jnp.where(hit, 1.0, hot)
            weighted = jnp.where(hit, scale, weighted)
        hot_ref[...] = hot.astype(BF)
        hot_out[...] = hot.astype(BF)
        total = jnp.sum(weighted, axis=1, keepdims=True)
        scale_out[...] = jnp.broadcast_to(total, scale_out.shape)

    values = jnp.concatenate([xa[:rows], xb[:rows]], axis=0)
    inputs = jnp.dot(hot_ref[...], values, preferred_element_type=F32)
    for m in range(n_key):
        out_ref[m] = inputs[m * slots : (m + 1) * slots].astype(BF)


def select(meta, count, mine, theirs, n_key, cap, top, tile, after):
    _, total, width = mine.shape
    rows = total - INFO_ROWS
    slots = 2 * cap
    tile = min(tile, width)
    at_info = rows // INFO_ROWS
    return pl.pallas_call(
        functools.partial(select_kernel, n_key, cap, top, rows),
        grid_spec=pltpu.PrefetchScalarGridSpec(
            num_scalar_prefetch=1,
            grid=(count, width // tile),
            in_specs=[
                pl.BlockSpec((None, total, tile), lambda j, i, meta: (meta[j + 1], 0, i)),
                pl.BlockSpec((None, total, tile), lambda j, i, meta: (meta[j + 1], 0, i)),
                pl.BlockSpec(
                    (None, INFO_ROWS, 4 * rows), lambda j, i, meta: (meta[j + 1], at_info, 0)
                ),
                pl.BlockSpec(
                    (None, INFO_ROWS, 4 * rows), lambda j, i, meta: (meta[j + 1], at_info, 0)
                ),
                ANY,
            ],
            out_specs=[
                pl.BlockSpec((n_key, None, slots, tile), lambda j, i, meta: (0, j, 0, i)),
                pl.BlockSpec((None, n_key * slots, 2 * rows), lambda j, i, meta: (j, 0, 0)),
                pl.BlockSpec((None, n_key * slots, 128), lambda j, i, meta: (j, 0, 0)),
            ],
            scratch_shapes=[pltpu.VMEM((n_key * slots, 2 * rows), BF)],
        ),
        out_shape=[
            jax.ShapeDtypeStruct((n_key, count, slots, width), BF),
            jax.ShapeDtypeStruct((count, n_key * slots, 2 * rows), BF),
            jax.ShapeDtypeStruct((count, n_key * slots, 128), F32),
        ],
        compiler_params=params(),
        cost_estimate=cost(),
        name="select_inputs",
    )(meta, mine, theirs, mine, theirs, after)


def scaled_kernel(n_key, meta, xa, xb, hot_ref, scale_ref, after, out_ref):
    slots = out_ref.shape[1]
    values = jnp.concatenate([xa[...], xb[...]], axis=0)
    rows = jnp.dot(hot_ref[...], values, preferred_element_type=F32) * scale_ref[:, :1]
    for m in range(n_key):
        out_ref[m] = rows[m * slots : (m + 1) * slots].astype(BF)


def select_scaled(meta, chunk, mine, theirs, hots, scales, n_key, tile, after):
    _, rows, width = mine.shape
    slots = hots.shape[1] // n_key
    tile = min(tile, width)
    block = pl.BlockSpec((None, rows, tile), lambda i, meta: (meta[chunk + 1], 0, i))
    return pl.pallas_call(
        functools.partial(scaled_kernel, n_key),
        grid_spec=pltpu.PrefetchScalarGridSpec(
            num_scalar_prefetch=1,
            grid=(width // tile,),
            in_specs=[
                block,
                block,
                pl.BlockSpec((None, n_key * slots, 2 * rows), lambda i, meta: (chunk, 0, 0)),
                pl.BlockSpec((None, n_key * slots, 128), lambda i, meta: (chunk, 0, 0)),
                ANY,
            ],
            out_specs=pl.BlockSpec((n_key, slots, tile), lambda i, meta: (0, 0, i)),
        ),
        out_shape=jax.ShapeDtypeStruct((n_key, slots, width), BF),
        compiler_params=params(),
        cost_estimate=cost(),
        name="select_scaled",
    )(meta, mine, theirs, hots, scales, after)


def gate_kernel(n_key, count, pieces, gate_w, up_w, *refs):
    in_ref, gate_ref, up_ref = refs[-3:]

    @pl.when(pl.program_id(0) == 0)
    def _():
        for j in range(count):
            joined = jnp.concatenate([pieces[m, j].astype(F32) for m in range(n_key)], axis=0)
            rows = joined.shape[0]
            in_ref[j * rows : (j + 1) * rows] = joined.astype(BF)

    gate_ref[...] = jnp.dot(in_ref[...], gate_w[...], preferred_element_type=F32)
    up_ref[...] = jnp.dot(in_ref[...], up_w[...], preferred_element_type=F32)


def gate_up(pieces, w_gate_up, hidden, tile, total, at, into, after):
    n_key, count, slots, width = pieces.shape
    rows = count * n_key * slots
    steps = hidden // tile
    part = pl.BlockSpec((rows, tile), lambda i: (0, i))
    return pl.pallas_call(
        functools.partial(gate_kernel, n_key, count),
        grid=(steps,),
        out_shape=[
            jax.ShapeDtypeStruct((total, width), BF),
            jax.ShapeDtypeStruct((rows, hidden), F32),
            jax.ShapeDtypeStruct((rows, hidden), F32),
        ],
        in_specs=[
            pl.BlockSpec((n_key, count, slots, width), lambda i: (0, 0, 0, 0)),
            pl.BlockSpec((width, tile), lambda i: (0, i)),
            pl.BlockSpec((width, tile), lambda i: (0, steps + i)),
            ANY,
        ]
        + [ANY] * len(into),
        out_specs=[pl.BlockSpec((rows, width), lambda i: (at, 0)), part, part],
        input_output_aliases={4 + i: i for i in range(len(into))},
        compiler_params=params(),
        cost_estimate=cost(),
        name="gate_up",
    )(pieces, w_gate_up, w_gate_up, after, *into)


def expert_kernel(n_key, meta, pieces, gate_in, up_in, gate_w, up_w, down_w, *refs):
    outs = refs[-n_key - 5 : -5]
    scaled_ref, hidden_ref, d_gate_ref, d_up_ref, total_ref = refs[-5:]
    slots = pieces.shape[1]
    step = pl.program_id(0)

    @pl.when(step == 0)
    def _():
        joined = jnp.concatenate([pieces[m].astype(F32) for m in range(n_key)], axis=0)
        scaled_ref[...] = joined.astype(BF)

    nt = (((1,), (1,)), ((), ()))
    gate, up = gate_in[...], up_in[...]
    d_hidden = lax.dot_general(scaled_ref[...], down_w[...], nt, preferred_element_type=F32)
    sigma = jax.nn.sigmoid(gate)
    activated = gate * sigma
    hidden_ref[...] = (activated * up).astype(BF)
    d_gate = (d_hidden * up * sigma * (1.0 + gate * (1.0 - sigma))).astype(BF)
    d_up = (d_hidden * activated).astype(BF)
    d_gate_ref[...] = d_gate
    d_up_ref[...] = d_up
    part = lax.dot_general(d_gate, gate_w[...], nt, preferred_element_type=F32)
    part = part + lax.dot_general(d_up, up_w[...], nt, preferred_element_type=F32)

    @pl.when(step == 0)
    def _():
        total_ref[...] = part

    @pl.when(step > 0)
    def _():
        total_ref[...] += part

    @pl.when(step == pl.num_programs(0) - 1)
    def _():
        for m in range(n_key):
            start = pl.multiple_of(jnp.bitwise_xor(meta[0], m) * slots, 8)
            outs[m][...] = total_ref[pl.ds(start, slots)].astype(BF)


def expert(meta, pieces, gate, up, chunk, w_gate_up, w_down, tile, at, chunks, kept, after):
    n_key, slots, width = pieces.shape
    hidden = w_down.shape[0]
    rows = n_key * slots
    steps = hidden // tile
    piece = pl.BlockSpec((n_key, slots, width), lambda i: (0, 0, 0))
    came = pl.BlockSpec((rows, tile), lambda i: (chunk, i))
    part = pl.BlockSpec((rows, tile), lambda i: (at, i))
    outs = pl.pallas_call(
        functools.partial(expert_kernel, n_key),
        grid=(steps,),
        out_shape=[jax.ShapeDtypeStruct((slots, width), BF)] * n_key
        + [jax.ShapeDtypeStruct((chunks * rows, width), BF)]
        + [jax.ShapeDtypeStruct((chunks * rows, hidden), BF)] * 3,
        in_specs=[
            pl.BlockSpec(memory_space=pltpu.SMEM),
            piece,
            came,
            came,
            pl.BlockSpec((width, tile), lambda i: (0, i)),
            pl.BlockSpec((width, tile), lambda i: (0, steps + i)),
            pl.BlockSpec((tile, width), lambda i: (i, 0)),
        ]
        + [ANY] * (len(kept) + 1),
        out_specs=[pl.BlockSpec((slots, width), lambda i: (0, 0))] * n_key
        + [pl.BlockSpec((rows, width), lambda i: (at, 0))]
        + [part] * 3,
        input_output_aliases={7 + i: n_key + i for i in range(len(kept))},
        scratch_shapes=[pltpu.VMEM((rows, width), F32)],
        compiler_params=params(),
        cost_estimate=cost(),
        name="expert_chunk",
    )(meta, pieces, gate, up, w_gate_up, w_gate_up, w_down, *kept, after)
    return list(outs[:n_key]), list(outs[n_key:])


def weights_kernel(left_ref, right_ref, *refs):
    out_ref, done_ref = refs[-2:]
    out_ref[...] = lax.dot_general(
        left_ref[...], right_ref[...], (((0,), (0,)), ((), ())), preferred_element_type=F32
    ).astype(BF)
    done_ref[...] = jnp.zeros_like(done_ref)


def weight_grad(left, right, tile, after, part=0, parts=1, into=None):
    rows, height = left.shape
    width = right.shape[1]
    aliased = [] if into is None else [into]
    return pl.pallas_call(
        weights_kernel,
        grid=(height // tile,),
        out_shape=[
            jax.ShapeDtypeStruct((height, parts * width), BF),
            jax.ShapeDtypeStruct((8, 128), F32),
        ],
        in_specs=[
            pl.BlockSpec((rows, tile), lambda i: (0, i)),
            pl.BlockSpec((rows, width), lambda i: (0, 0)),
            ANY,
        ]
        + [ANY] * len(aliased),
        out_specs=[
            pl.BlockSpec((tile, width), lambda i: (i, part)),
            pl.BlockSpec((8, 128), lambda i: (0, 0)),
        ],
        input_output_aliases={3: 0} if aliased else {},
        compiler_params=params(),
        cost_estimate=cost(),
        name="weight_gradient",
    )(left, right, after, *aliased)


def combine_kernel(n_key, meta, hot_ref, *refs):
    backs = refs[:n_key]
    keep_ref, send_ref, joined_ref = refs[n_key + 1 :]
    rows = keep_ref.shape[0]
    slots = backs[0].shape[0]
    tn = (((0,), (0,)), ((), ()))
    for m in range(n_key):
        start = pl.multiple_of(jnp.bitwise_xor(meta[0], m) * slots, 8)
        joined_ref[pl.ds(start, slots)] = backs[m][...].astype(F32)
    total = lax.dot_general(
        hot_ref[...], joined_ref[...].astype(BF), tn, preferred_element_type=F32
    )
    keep_ref[...] = total[:rows]
    send_ref[...] = total[rows:].astype(BF)


def combine(meta, hots, chunk, backs, tile, after):
    n_key = len(backs)
    slots, width = backs[0].shape
    tokens = hots.shape[2]
    rows = tokens // 2
    tile = min(tile, width)
    return pl.pallas_call(
        functools.partial(combine_kernel, n_key),
        grid=(width // tile,),
        out_shape=[
            jax.ShapeDtypeStruct((rows, width), F32),
            jax.ShapeDtypeStruct((rows, width), BF),
        ],
        in_specs=[
            pl.BlockSpec(memory_space=pltpu.SMEM),
            pl.BlockSpec((None, n_key * slots, tokens), lambda i: (chunk, 0, 0)),
        ]
        + [pl.BlockSpec((slots, tile), lambda i: (0, i))] * n_key
        + [ANY],
        out_specs=[pl.BlockSpec((rows, tile), lambda i: (0, i))] * 2,
        scratch_shapes=[pltpu.VMEM((n_key * slots, tile), F32)],
        compiler_params=params(),
        cost_estimate=cost(),
        name="combine_rows",
    )(meta, hots, *backs, after)


ORDER = ((3, 1, 2), (3, 2, 0), (3, 0, 1), (0, 1, 2))


def layer(tokens, upstream, route_weight, expert_ids, w_gate_up, w_down, early, attend):
    n_key = lax.axis_size("key")
    n_z = lax.axis_size("z")
    tok_dev = tokens.shape[0]
    top_count = expert_ids.shape[1]
    cap = max(2, 9 * tok_dev * top_count // (16 * n_z * n_key))
    head = lax.axis_index(HEAD)
    core = lax.axis_index("core")
    z = lax.axis_index("z")
    key = lax.axis_index("key")
    key_meta = key.astype(jnp.int32)[None]
    rows = n_key * 2 * cap
    hidden_width = w_down.shape[0]
    block = build(expert_ids.T, route_weight.T, tokens)
    column = lax.all_gather(block, "z")
    column_up = lax.all_gather(upstream, "z")
    state = {"after": block}
    hots, backs, parts, kept, totals = {}, {}, {}, [], {}

    def after(x, *others):
        return lax.optimization_barrier((x, *others))[0]

    def exchange(x):
        return lax.all_to_all(x, "key", split_axis=0, concat_axis=0, tiled=True)

    def run_inputs(heights, mine, theirs):
        meta = jnp.stack([head * n_key] + heights).astype(jnp.int32)
        out = select(
            meta, len(heights), mine, theirs, n_key, cap, top_count, 1024, state["after"]
        )
        state["after"] = out[1]
        return (meta, *out)

    def run_scaled(meta, chunk, mine, theirs, hots, scales):
        out = select_scaled(
            meta,
            chunk,
            mine,
            theirs,
            hots,
            scales,
            n_key,
            1024,
            state["after"],
        )
        state["after"] = out
        return exchange(out)

    def run_gate(pieces, at, into, tile):
        out = gate_up(
            pieces, w_gate_up, hidden_width, tile, n_z * rows, at, into, state["after"]
        )
        state["after"] = out[1]
        return out

    def run_expert(m, pieces, gate, up):
        out, kept[:] = expert(
            key_meta,
            pieces,
            gate,
            up,
            max(m - 1, 0),
            w_gate_up,
            w_down,
            hidden_width,
            (m - 1) % n_z,
            n_z,
            list(kept),
            state["after"],
        )
        state["after"] = out[0]
        backs[m] = [out[0]] + [swap(out[i], "key", i) for i in range(1, n_key)]

    def run_combine(m):
        parts[m] = combine(
            key_meta, hots[min(m, 1)], max(m - 1, 0), backs[m], 1024, state["after"]
        )
        state["after"] = parts[m][0]

    def run_total(m):
        keep, send = parts[m]
        totals[m] = keep + swap(send, "core", 1).astype(F32)
        totals[m] = totals[m] if m == 0 else totals[m].astype(BF)

    def pass_z(block, route):
        return lax.ppermute(block, "z", route)

    def then(*others):
        state["after"] = after(state["after"], *others)

    near, near2 = block[None], swap(block, "core", 1)[None]
    meta, inputs, hots[0], scales = run_inputs([z * 0], near, near2)
    inputs = exchange(inputs)
    near, near2 = upstream[None], swap(upstream, "core", 1)[None]
    scaled = run_scaled(meta, 0, near, near2, hots[0], scales)
    ins, gate, up = run_gate(inputs, n_z - 1, [], 384)
    run_expert(0, scaled, gate, up)
    column = after(column, state["after"], *early)
    heights = [pick(z, [jnp.int32(order[j]) for order in ORDER]) for j in range(n_z - 1)]
    meta, inputs, hots[1], scales = run_inputs(heights, column, swap(column, "core", 1))
    inputs = exchange(after(inputs, *backs[0]))
    column_up = after(column_up, state["after"])
    column_up2 = swap(column_up, "core", 1)
    scaled = {}

    def fetch_scaled(m):
        scaled[m] = run_scaled(meta, m - 1, column_up, column_up2, hots[1], scales)

    fetch_scaled(1)
    ins, gate, up = run_gate(inputs, 0, [ins], 256)
    fetch_scaled(2)
    run_expert(1, scaled[1], gate, up)
    fetch_scaled(3)
    run_combine(0)
    run_expert(2, scaled[2], gate, up)
    then(scaled[3])
    run_combine(1)

    last = z == n_z - 1
    partial = jnp.where(head * n_key + key == 2 * n_z * n_key - 1, upstream.astype(F32), 0.0)
    for m, there in ((0, last), (1, jnp.logical_not(last))):
        keep, send = parts[m]
        partial = partial + jnp.where(there, jnp.where(core == 1, keep, send.astype(F32)), 0.0)
    half = partial.shape[1] // 2
    first = core == 0
    lower, upper = partial[:, :half], partial[:, half:]
    held = jnp.where(first, lower, upper)
    held = held + swap(jnp.where(first, upper, lower).astype(BF), "core", 1).astype(F32)
    held = held.astype(BF)
    run_total(0)
    run_total(1)
    arrived_a = pass_z(totals[1], [(0, 3), (3, 0)])
    then(held)
    run_expert(3, scaled[3], gate, up)
    held = (held.astype(F32) + swap(held, "z", 1).astype(F32)).astype(BF)
    then(held)
    run_combine(2)
    run_total(2)
    arrived_b = pass_z(jnp.where(last, totals[2], totals[1]), [(1, 3), (3, 1)])
    arrived_d = pass_z(totals[2], [(0, 1), (1, 2), (2, 0)])
    held = (held.astype(F32) + swap(held, "z", 2).astype(F32)).astype(BF)
    held = jnp.where(key == n_key - 1, held, jnp.zeros_like(held))
    scaled, hidden, d_gate, d_up = kept
    grad_down, state["after"] = weight_grad(hidden, scaled, 384, state["after"])
    then(held)
    run_combine(3)
    run_total(3)
    arrived_c = pass_z(jnp.where(last, totals[3], totals[1]), [(2, 3), (3, 2)])
    arrived_e = pass_z(totals[3], [(0, 2), (1, 0), (2, 1)])
    sources = [n_key - 1]
    bit = 1
    while bit < n_key:
        route = [(i, i ^ bit) for i in sources]
        held = held + lax.ppermute(held, "key", route)
        sources += [target for _, target in route]
        bit *= 2
    then(held)
    grads, state["after"] = weight_grad(ins, d_gate, 512, state["after"], 0, 2)
    other = swap(held, "core", 1)
    window = jnp.concatenate(
        [jnp.where(first, held, other), jnp.where(first, other, held)], axis=1
    )
    outs, done = attend(window)
    then(arrived_a, arrived_b, arrived_d, *done)
    grads, state["after"] = weight_grad(ins, d_up, 512, state["after"], 1, 2, grads)
    resid = upstream.astype(F32) + totals[0]
    for arrived in (arrived_a, arrived_b, arrived_d):
        resid = resid + arrived.astype(F32)
    for arrived in (arrived_c, arrived_e):
        resid = resid + after(arrived, state["after"]).astype(F32)
    return (resid.astype(BF), grads, grad_down, *outs)


def shards(
    tokens,
    upstream,
    route_weight,
    expert_ids,
    w_gate_up,
    w_down,
    w_out,
    queries,
    keys_values,
    key_blocks,
    attn_out,
    attn_lse,
):
    tok_dev, d_model = tokens.shape
    n_head = lax.axis_size(HEAD)
    n_key = lax.axis_size("key")
    head = lax.axis_index(HEAD)
    key = lax.axis_index("key")
    core = head % 2
    query_len = queries.shape[0]
    heads_dev = queries.shape[1] // HD
    key_dev = keys_values.shape[0]
    total_keys = key_dev * n_key
    score_scale = HD ** (-0.5)

    def by_head(x):
        return x.reshape(query_len, heads_dev, HD).transpose(1, 0, 2).reshape(-1, HD)

    kv_head = head * heads_dev // (QH // KVH)
    key_head = lax.dynamic_slice_in_dim(keys_values, kv_head * HD, HD, 1)
    value_head = lax.dynamic_slice_in_dim(keys_values, (KVH + kv_head) * HD, HD, 1)
    query_rows = by_head(queries)
    out_rows = by_head(attn_out)
    key_pos = (key_blocks[:, None] * KBLK + jnp.arange(KBLK, dtype=jnp.int32)[None, :]).reshape(
        key_dev
    )
    query_pos = total_keys - query_len + jnp.arange(query_len, dtype=jnp.int32)
    visible = key_pos[None, :] <= jnp.tile(query_pos, heads_dev)[:, None]
    scores = dot(query_rows, key_head, ((1,), (1,))) * score_scale
    probs = jnp.where(visible, jnp.exp(scores - attn_lse.reshape(-1)[:, None]), 0.0)

    def attend(window):
        d_attn = dot(window, w_out, ((1,), (1,))).astype(BF)
        column_width = d_model // n_key
        columns = lax.dynamic_slice_in_dim(window, key * column_width, column_width, 1)
        grad_out = dot(attn_out, columns, ((0,), (0,))).astype(BF)
        grad_rows = by_head(d_attn)
        delta = jnp.sum(grad_rows.astype(F32) * out_rows.astype(F32), axis=1)
        d_probs = dot(grad_rows, value_head, ((1,), (1,)))
        d_scores = (probs * (d_probs - delta[:, None])).astype(BF)
        d_query = dot(d_scores, key_head, ((1,), (0,))) * score_scale
        d_key = dot(d_scores, query_rows, ((0,), (0,))) * score_scale
        d_value = dot(probs.astype(BF), grad_rows, ((0,), (0,)))

        first = core == 0
        held = jnp.where(first, d_key, d_value)
        other = jnp.where(first, d_value, d_key).astype(BF)
        held = (held + swap(other, "core", 1).astype(F32)).astype(BF)
        to_owner = [(i, i % 2 * KVH + i // 2) for i in range(n_head)]
        d_keys_values = lax.ppermute(held, HEAD, to_owner)

        d_query = d_query.reshape(heads_dev, query_len, HD).transpose(1, 0, 2)
        d_query = d_query.reshape(query_len, heads_dev * HD)
        share = query_len // n_key
        d_queries = lax.dynamic_slice_in_dim(d_query, key * share, share, 0)
        for m in range(1, n_key):
            part = lax.dynamic_slice_in_dim(d_query, jnp.bitwise_xor(key, m) * share, share, 0)
            d_queries = d_queries + swap(part, "key", m)
        return (grad_out, d_queries.astype(BF), d_keys_values), (d_query, held, grad_out)

    slots = 2 * max(2, 9 * tok_dev * expert_ids.shape[1] // (8 * n_head * n_key))
    run_layer = layer if slots % 8 == 0 and n_head == 2 * len(ORDER) else layer_plain
    d_resid, grad_gate_up, grad_down, *rest = run_layer(
        tokens,
        upstream,
        route_weight,
        expert_ids,
        w_gate_up[0],
        w_down[0],
        (probs, query_rows, out_rows),
        attend,
    )
    return (d_resid, grad_gate_up[None], grad_down[None], *rest)


def solution(mesh):
    sizes = mesh.devices.shape
    parts = jax.sharding.Mesh(
        mesh.devices.reshape(sizes[0] // 2, 2, sizes[1]), ("z", "core", "key")
    )
    every = ("z", "core", "key")
    return jax.shard_map(
        shards,
        mesh=parts,
        in_specs=(
            P(every, None),
            P(every, None),
            P(every, None),
            P(every, None),
            P(every, None, None),
            P(every, None, None),
            P(HEAD, None),
            P(None, HEAD),
            P("key", None),
            P("key"),
            P(None, HEAD),
            P(HEAD, None),
        ),
        out_specs=(
            P(every, None),
            P(every, None, None),
            P(every, None, None),
            P(HEAD, "key"),
            P("key", HEAD),
            P("key", HEAD),
        ),
        check_vma=False,
    )
```

profile of v0, /device:TPU:0, one launch (start us, length us, event | category | flops | bytes accessed | tf_op | source)
XLA Modules:
  0.0 339.7 jit_solution(8578285246395339090)
XLA Ops:
  7.2 2.1 build_block.1.after
  12.5 3.7 %select_inputs.2 = (bf16[4,1,72,2048]{3,2,1,0:T(8,128)(2,1)}, bf16[1,288,256]{2,1,0:T(8,128)(2,1)}, f32[1,288,128]{2,1,0:T(8,128)}) custom-call(s32[2]{0:T(128)} %pad_add_fusion.meta, bf16[1,144,2048]{2,1,0:T(8,128)(2,1)} %bitcast.83, bf16[1,144,2048]{2,1,0:T(8,128)(2,1)} %bitcast.90, bf16[1,144,2048]{2,1,0:T(8,128)(2,1)} %bitcast.84, ...), custom_call_target="tpu_custom_call" | custom-call | flops 1000 | bytes 1000 | tf_op jit(solution)/shard_map/select_inputs/pallas_call | solution.py:304
  16.2 5.1 %all-to-all-start.1 = ((bf16[4,1,72,2048]{3,2,1,0:T(8,128)(2,1)}), bf16[4,1,72,2048]{3,2,1,0:T(8,128)(2,1)}, u32[]{:S(2)}, u32[]{:S(2)}) async-start(bf16[4,1,72,2048]{3,2,1,0:T(8,128)(2,1)} %get-tuple-element.77), calls=%async_computation.1 | async-start | bytes 2359296 | tf_op jit(solution)/shard_map/all_to_all | solution.py:594
  24.1 3.4 %select_scaled.4.refs_0_ = bf16[4,72,2048]{2,1,0:T(8,128)(2,1)} custom-call(s32[2]{0:T(128)} %pad_add_fusion.meta, bf16[1,128,2048]{2,1,0:T(8,128)(2,1)} %bitcast.88, bf16[1,128,2048]{2,1,0:T(8,128)(2,1)} %bitcast.99, bf16[1,288,256]{2,1,0:T(8,128)(2,1)} %get-tuple-element.75.hot_ref.after, f32[1,288,128]{2,1,0:T(8,128)} %get-tuple-element.76.scale_ref, ...), custom_call_target="tpu_custom_call" | custom-call | flops 1000 | bytes 1000 | tf_op jit(solution)/shard_map/select_scaled/pallas_call | solution.py:351
  27.5 9.8 %all-to-all-done.1.pieces = bf16[4,1,72,2048]{3,2,1,0:T(8,128)(2,1)} async-done(((bf16[4,1,72,2048]{3,2,1,0:T(8,128)(2,1)}), bf16[4,1,72,2048]{3,2,1,0:T(8,128)(2,1)}, u32[]{:S(2)}, u32[]{:S(2)}) %all-to-all-start.1) | async-done | bytes 1179680 | tf_op jit(solution)/shard_map/all_to_all | solution.py:594
  37.4 3.5 %all-to-all-start = ((bf16[4,72,2048]{2,1,0:T(8,128)(2,1)}), bf16[4,72,2048]{2,1,0:T(8,128)(2,1)S(1)}, u32[]{:S(2)}, u32[]{:S(2)}) async-start(bf16[4,72,2048]{2,1,0:T(8,128)(2,1)} %select_scaled.4.refs_0_), calls=%async_computation | async-start | bytes 2359296 | tf_op jit(solution)/shard_map/all_to_all | solution.py:594
  43.3 6.0 %gate_up.2 = (bf16[1152,2048]{1,0:T(8,128)(2,1)}, f32[288,768]{1,0:T(8,128)}, f32[288,768]{1,0:T(8,128)}) custom-call(bf16[4,1,72,2048]{3,2,1,0:T(8,128)(2,1)} %all-to-all-done.1.pieces, bf16[2048,1536]{1,0:T(8,128)(2,1)} %bitcast.63, bf16[2048,1536]{1,0:T(8,128)(2,1)} %bitcast.64, bf16[4,72,2048]{2,1,0:T(8,128)(2,1)} %select_scaled.4.refs_0_), custom_call_target="tpu_custom_call" | custom-call | flops 1000 | bytes 1000 | tf_op jit(solution)/shard_map/gate_up/pallas_call | solution.py:391
  49.2 6.7 %all-to-all-done.pieces = bf16[4,72,2048]{2,1,0:T(8,128)(2,1)S(1)} async-done(((bf16[4,72,2048]{2,1,0:T(8,128)(2,1)}), bf16[4,72,2048]{2,1,0:T(8,128)(2,1)S(1)}, u32[]{:S(2)}, u32[]{:S(2)}) %all-to-all-start) | async-done | bytes 1179680 | tf_op jit(solution)/shard_map/all_to_all | solution.py:594
  57.0 10.2 %expert_chunk.4 = (bf16[72,2048]{1,0:T(8,128)(2,1)}, bf16[72,2048]{1,0:T(8,128)(2,1)}, bf16[72,2048]{1,0:T(8,128)(2,1)}, bf16[72,2048]{1,0:T(8,128)(2,1)}, bf16[...) custom-call(s32[1]{0:T(128)} %bitcast.meta, ...), custom_call_target="tpu_custom_call" | custom-call | flops 1000 | bytes 1000 | tf_op jit(solution)/shard_map/expert_chunk/pallas_call | solution.py:461
  72.2 7.7 %select_inputs.3 = (bf16[4,3,72,2048]{3,2,1,0:T(8,128)(2,1)}, bf16[3,288,256]{2,1,0:T(8,128)(2,1)}, f32[3,288,128]{2,1,0:T(8,128)}) custom-call(s32[4]{0:T(128)} %pad_add_fusion.1.meta, bf16[4,144,2048]{2,1,0:T(8,128)(2,1)} %bitcast.86, bf16[4,144,2048]{2,1,0:T(8,128)(2,1)} %collective-permute-done.5.xb.ib, bf16[4,144,2048]{2,1,0:T(8,128)(2,1)} %bitcast.87, ...), custom_call_target="tpu_custom_call" | custom-call | flops 1000 | bytes 1000 | tf_op jit(solution)/shard_map/select_inputs/pallas_call | solution.py:304
  79.9 4.5 %collective-permute-done.3.refs_2_ = bf16[72,2048]{1,0:T(8,128)(2,1)S(1)} collective-permute-done((bf16[72,2048]{1,0:T(8,128)(2,1)}, bf16[72,2048]{1,0:T(8,128)(2,1)S(1)}, u32[]{:S(2)}, u32[]{:S(2)}) %collective-permute-start.3) | collective-permute-done | bytes 294944 | tf_op jit(solution)/shard_map/ppermute | solution.py:28
  85.2 4.7 %all-to-all-start.3 = ((bf16[4,3,72,2048]{3,2,1,0:T(8,128)(2,1)}), bf16[4,3,72,2048]{3,2,1,0:T(8,128)(2,1)}, u32[]{:S(2)}, u32[]{:S(2)}) async-start(bf16[4,3,72,2048]{3,2,1,0:T(8,128)(2,1)} %get-tuple-element.89), calls=%async_computation.3 | async-start | bytes 7077888 | tf_op jit(solution)/shard_map/all_to_all | solution.py:594
  90.0 19.1 %all-gather.5.cloned.1.call-done = bf16[512,2048]{1,0:T(8,128)(2,1)} async-done(((bf16[128,2048]{1,0:T(8,128)(2,1)}), bf16[512,2048]{1,0:T(8,128)(2,1)}) %all-gather.5.cloned.1.call-update) | async-done | bytes 2097168 | tf_op jit(solution)/shard_map/all_gather | solution.py:586
  109.1 4.4 %collective-permute-done.6.xb = bf16[4,128,2048]{2,1,0:T(8,128)(2,1)S(1)} collective-permute-done((bf16[4,128,2048]{2,1,0:T(8,128)(2,1)}, bf16[4,128,2048]{2,1,0:T(8,128)(2,1)S(1)}, u32[]{:S(2)}, u32[]{:S(2)}) %collective-permute-start.6) | collective-permute-done | bytes 2097184 | tf_op jit(solution)/shard_map/ppermute | solution.py:28
  114.7 3.3 select_scaled.5.refs_0_
  118.1 12.2 %all-to-all-done.3.pieces = bf16[4,3,72,2048]{3,2,1,0:T(8,128)(2,1)} async-done(((bf16[4,3,72,2048]{3,2,1,0:T(8,128)(2,1)}), bf16[4,3,72,2048]{3,2,1,0:T(8,128)(2,1)}, u32[]{:S(2)}, u32[]{:S(2)}) %all-to-all-start.3) | async-done | bytes 3538976 | tf_op jit(solution)/shard_map/all_to_all | solution.py:594
  130.3 3.5 %all-to-all-start.2 = ((bf16[4,72,2048]{2,1,0:T(8,128)(2,1)}), bf16[4,72,2048]{2,1,0:T(8,128)(2,1)S(1)}, u32[]{:S(2)}, u32[]{:S(2)}) async-start(bf16[4,72,2048]{2,1,0:T(8,128)(2,1)} %select_scaled.5.refs_0_), calls=%async_computation.2 | async-start | bytes 2359296 | tf_op jit(solution)/shard_map/all_to_all | solution.py:594
  133.8 10.4 %gate_up.3 = (bf16[1152,2048]{1,0:T(8,128)(2,1)}, f32[864,768]{1,0:T(8,128)}, f32[864,768]{1,0:T(8,128)}) custom-call(bf16[4,3,72,2048]{3,2,1,0:T(8,128)(2,1)} %all-to-all-done.3.pieces, bf16[2048,1536]{1,0:T(8,128)(2,1)} %bitcast.67, bf16[2048,1536]{1,0:T(8,128)(2,1)} %bitcast.68, ...), custom_call_target="tpu_custom_call", output_to_operand_aliasing={{0}: (4, {})} | custom-call | flops 1000 | bytes 1000 | tf_op jit(solution)/shard_map/gate_up/pallas_call | solution.py:391
  144.2 3.3 select_scaled.6.refs_4_
  149.3 3.7 %all-to-all-start.4 = ((bf16[4,72,2048]{2,1,0:T(8,128)(2,1)}), bf16[4,72,2048]{2,1,0:T(8,128)(2,1)S(1)}, u32[]{:S(2)}, u32[]{:S(2)}) async-start(bf16[4,72,2048]{2,1,0:T(8,128)(2,1)} %select_scaled.6.refs_4_), calls=%async_computation.4 | async-start | bytes 2359296 | tf_op jit(solution)/shard_map/all_to_all | solution.py:594
  153.0 10.0 %expert_chunk.5 = (bf16[72,2048]{1,0:T(8,128)(2,1)}, bf16[72,2048]{1,0:T(8,128)(2,1)}, bf16[72,2048]{1,0:T(8,128)(2,1)}, bf16[72,2048]{1,0:T(8,128)(2,1)}, bf16[...) custom-call(s32[1]{0:T(128)} %bitcast.meta, ...), custom_call_target="tpu_custom_call", output_to_operand_aliasing={{4}: (7, {}), {5}: (8, {}), {6}: (9, {}), {7}: (10, {})} | custom-call | flops 1000 | bytes 1000 | tf_op jit(solution)/shard_map/expert_chunk/pallas_call | solution.py:461
  163.0 3.3 select_scaled.7.refs_4_
  167.3 4.3 %all-to-all-start.5 = ((bf16[4,72,2048]{2,1,0:T(8,128)(2,1)}), bf16[4,72,2048]{2,1,0:T(8,128)(2,1)}, u32[]{:S(2)}, u32[]{:S(2)}) async-start(bf16[4,72,2048]{2,1,0:T(8,128)(2,1)} %select_scaled.7.refs_4_), calls=%async_computation.5 | async-start | bytes 2359296 | tf_op jit(solution)/shard_map/all_to_all | solution.py:594
  171.6 2.9 collective-permute-start.10
  175.1 3.2 combine_rows.4
  178.3 9.9 %expert_chunk.6 = (bf16[72,2048]{1,0:T(8,128)(2,1)}, bf16[72,2048]{1,0:T(8,128)(2,1)}, bf16[72,2048]{1,0:T(8,128)(2,1)}, bf16[72,2048]{1,0:T(8,128)(2,1)}, bf16[...) custom-call(s32[1]{0:T(128)} %bitcast.meta, ...), custom_call_target="tpu_custom_call", output_to_operand_aliasing={{4}: (7, {}), {5}: (8, {}), {6}: (9, {}), {7}: (10, {})} | custom-call | flops 1000 | bytes 1000 | tf_op jit(solution)/shard_map/expert_chunk/pallas_call | solution.py:461
  188.2 3.3 all-to-all-done.5.pieces
  191.5 3.8 %collective-permute-done.10.refs_3_ = bf16[72,2048]{1,0:T(8,128)(2,1)} collective-permute-done((bf16[72,2048]{1,0:T(8,128)(2,1)}, bf16[72,2048]{1,0:T(8,128)(2,1)}, u32[]{:S(2)}, u32[]{:S(2)}) %collective-permute-start.10) | collective-permute-done | bytes 294944 | tf_op jit(solution)/shard_map/ppermute | solution.py:28
  195.3 3.4 %collective-permute-done.8.refs_1_ = bf16[72,2048]{1,0:T(8,128)(2,1)} collective-permute-done((bf16[72,2048]{1,0:T(8,128)(2,1)}, bf16[72,2048]{1,0:T(8,128)(2,1)}, u32[]{:S(2)}, u32[]{:S(2)}) %collective-permute-start.8) | collective-permute-done | bytes 294944 | tf_op jit(solution)/shard_map/ppermute | solution.py:28
  198.8 3.2 combine_rows.5
  210.4 3.4 collective-permute-done.17
  213.9 2.5 collective-permute-start.24
  216.3 10.0 %expert_chunk.7 = (bf16[72,2048]{1,0:T(8,128)(2,1)}, bf16[72,2048]{1,0:T(8,128)(2,1)}, bf16[72,2048]{1,0:T(8,128)(2,1)}, bf16[72,2048]{1,0:T(8,128)(2,1)}, bf16[...) custom-call(s32[1]{0:T(128)} %bitcast.meta, ...), custom_call_target="tpu_custom_call", output_to_operand_aliasing={{4}: (7, {}), {5}: (8, {}), {6}: (9, {}), {7}: (10, {})} | custom-call | flops 1000 | bytes 1000 | tf_op jit(solution)/shard_map/expert_chunk/pallas_call | solution.py:461
  229.8 3.2 combine_rows.6
  233.0 8.2 %weight_gradient.3 = (bf16[768,2048]{1,0:T(8,128)(2,1)}, f32[8,128]{1,0:T(8,128)}) custom-call(bf16[1152,768]{1,0:T(8,128)(2,1)} %get-tuple-element.126.left_ref, bf16[1152,2048]{1,0:T(8,128)(2,1)} %get-tuple-element.127.right_ref, f32[128,2048]{1,0:T(8,128)} %get-tuple-element.121.refs_0_), custom_call_target="tpu_custom_call" | custom-call | flops 1000 | bytes 1000 | tf_op jit(solution)/shard_map/weight_gradient/pallas_call | solution.py:501
  243.0 3.2 combine_rows.7
  250.9 11.2 %collective-permute-done.28 = bf16[128,1024]{1,0:T(8,128)(2,1)} collective-permute-done((bf16[128,1024]{1,0:T(8,128)(2,1)S(1)}, bf16[128,1024]{1,0:T(8,128)(2,1)}, u32[]{:S(2)}, u32[]{:S(2)}) %collective-permute-start.28) | collective-permute-done | bytes 262176 | tf_op jit(solution)/shard_map/ppermute | solution.py:724
  263.2 3.2 broadcast_select_fusion
  266.4 2.4 broadcast_select_fusion.1
  275.8 3.5 %collective-permute-start.34 = (f32[32,512]{1,0:T(8,128)}, f32[32,512]{1,0:T(8,128)}, u32[]{:S(2)}, u32[]{:S(2)}) collective-permute-start(f32[32,512]{1,0:T(8,128)} %get-tuple-element.170), channel_id=1, source_target_pairs={{0,3},{1,2},{2,1},{3,0},{4,7},{5,6},{6,5},{7,4},{8,11},{9,10},{10,... | collective-permute-start | bytes 196616 | tf_op jit(solution)/shard_map/ppermute | solution.py:28
  279.3 8.1 %weight_gradient.4 = (bf16[2048,1536]{1,0:T(8,128)(2,1)}, f32[8,128]{1,0:T(8,128)}) custom-call(bf16[1152,2048]{1,0:T(8,128)(2,1)} %get-tuple-element.132.left_ref, bf16[1152,768]{1,0:T(8,128)(2,1)} %get-tuple-element.134.right_ref, f32[128,2048]{1,0:T(8,128)} %get-tuple-element.135.refs_0_), custom_call_target="tpu_custom_call" | custom-call | flops 1000 | bytes 1000 | tf_op jit(solution)/shard_map/weight_gradient/pallas_call | solution.py:501
  287.4 6.1 %collective-permute-start.12 = (bf16[128,2048]{1,0:T(8,128)(2,1)}, bf16[128,2048]{1,0:T(8,128)(2,1)}, u32[]{:S(2)}, u32[]{:S(2)}) collective-permute-start(bf16[128,2048]{1,0:T(8,128)(2,1)} %get-tuple-element.163), channel_id=1, source_target_pairs={{0,24},{24,0},{1,25},{25,1},{2,26},{26,2},{3,27},{27,3},{4,28},{28... | collective-permute-start | bytes 1572872 | tf_op jit(solution)/shard_map/ppermute | solution.py:656
  297.0 5.3 %collective-permute-start.31 = (bf16[128,2048]{1,0:T(8,128)(2,1)}, bf16[128,2048]{1,0:T(8,128)(2,1)}, u32[]{:S(2)}, u32[]{:S(2)}) collective-permute-start(bf16[128,2048]{1,0:T(8,128)(2,1)} %get-tuple-element.164), channel_id=1, source_target_pairs={{0,16},{8,0},{16,8},{1,17},{9,1},{17,9},{2,18},{10,2},{18,10},{3,1... | collective-permute-start | bytes 1572872 | tf_op jit(solution)/shard_map/ppermute | solution.py:656
  303.5 2.0 copy.46
  308.2 9.5 %collective-permute-done.20 = bf16[128,2048]{1,0:T(8,128)(2,1)} collective-permute-done((bf16[128,2048]{1,0:T(8,128)(2,1)}, bf16[128,2048]{1,0:T(8,128)(2,1)}, u32[]{:S(2)}, u32[]{:S(2)}) %collective-permute-start.20) | collective-permute-done | bytes 524320 | tf_op jit(solution)/shard_map/ppermute | solution.py:656
  318.5 8.1 %weight_gradient.5 = (bf16[2048,1536]{1,0:T(8,128)(2,1)}, f32[8,128]{1,0:T(8,128)}) custom-call(bf16[1152,2048]{1,0:T(8,128)(2,1)} %get-tuple-element.132.left_ref, bf16[1152,768]{1,0:T(8,128)(2,1)} %get-tuple-element.133.right_ref, f32[8,128]{1,0:T(8,128)} %get-tuple-element.137.refs_0_, ...), custom_call_target="tpu_custom_call", output_to_operand_aliasing={{0}: (3, {})} | custom-call | flops 1000 | bytes 1000 | tf_op jit(solution)/shard_map/weight_gradient/pallas_call | solution.py:501
  326.6 2.3 collective-permute-done.31
  328.9 3.3 fusion.7
  (160 shorter events, 54.6 us)
Async XLA Ops:
  7.2 34.2 %copy-start = (bf16[1024,1024]{1,0:T(8,128)(2,1)S(1)}, bf16[1024,1024]{1,0:T(8,128)(2,1)}, u32[]{:S(2)}) copy-start(bf16[1024,1024]{1,0:T(8,128)(2,1)} %param.20) | copy-start | bytes 6291460
  7.2 60.0 %all-gather.7.cloned.1.call-start = ((), (), s32[]{:S(2)}) async-start(), calls=%async_computation.7 | async-start | bytes 2949120 | tf_op jit(solution)/shard_map/all_gather | solution.py:585
  9.3 2.4 collective-permute-start
  16.2 21.1 %all-to-all-start.1 = ((bf16[4,1,72,2048]{3,2,1,0:T(8,128)(2,1)}), bf16[4,1,72,2048]{3,2,1,0:T(8,128)(2,1)}, u32[]{:S(2)}, u32[]{:S(2)}) async-start(bf16[4,1,72,2048]{3,2,1,0:T(8,128)(2,1)} %get-tuple-element.77), calls=%async_computation.1 | async-start | bytes 2359296 | tf_op jit(solution)/shard_map/all_to_all | solution.py:594
  21.3 87.8 %all-gather.5.cloned.1.call-start = ((), (), s32[]{:S(2)}) async-start(), calls=%async_computation.6 | async-start | bytes 2621440 | tf_op jit(solution)/shard_map/all_gather | solution.py:586
  21.3 2.0 collective-permute-start.1
  24.1 16.9 %copy-start.25 = (bf16[128,512]{1,0:T(8,128)(2,1)S(1)}, bf16[128,512]{1,0:T(8,128)(2,1)}, u32[]{:S(2)}) copy-start(bf16[128,512]{1,0:T(8,128)(2,1)} %param.19) | copy-start | bytes 393220
  37.4 18.6 %all-to-all-start = ((bf16[4,72,2048]{2,1,0:T(8,128)(2,1)}), bf16[4,72,2048]{2,1,0:T(8,128)(2,1)S(1)}, u32[]{:S(2)}, u32[]{:S(2)}) async-start(bf16[4,72,2048]{2,1,0:T(8,128)(2,1)} %select_scaled.4.refs_0_), calls=%async_computation | async-start | bytes 2359296 | tf_op jit(solution)/shard_map/all_to_all | solution.py:594
  67.2 4.9 %collective-permute-start.5 = (bf16[4,144,2048]{2,1,0:T(8,128)(2,1)}, bf16[4,144,2048]{2,1,0:T(8,128)(2,1)}, u32[]{:S(2)}, u32[]{:S(2)}) collective-permute-start(bf16[4,144,2048]{2,1,0:T(8,128)(2,1)} %bitcast.85), channel_id=1, source_target_pairs={{0,4},{4,0},{1,5},{5,1},{2,6},{6,2},{3,7},{7,3},{8,12},{12,8},{9,1... | collective-permute-start | bytes 7077896 | tf_op jit(solution)/shard_map/ppermute | solution.py:28
  67.3 12.6 %collective-permute-start.2 = (bf16[72,2048]{1,0:T(8,128)(2,1)}, bf16[72,2048]{1,0:T(8,128)(2,1)S(1)}, u32[]{:S(2)}, u32[]{:S(2)}) collective-permute-start(bf16[72,2048]{1,0:T(8,128)(2,1)} %get-tuple-element.81), channel_id=1, source_target_pairs={{0,1},{1,0},{2,3},{3,2},{4,5},{5,4},{6,7},{7,6},{8,9},{9,8},{10,11... | collective-permute-start | bytes 884744 | tf_op jit(solution)/shard_map/ppermute | solution.py:28
  68.8 15.6 %collective-permute-start.3 = (bf16[72,2048]{1,0:T(8,128)(2,1)}, bf16[72,2048]{1,0:T(8,128)(2,1)S(1)}, u32[]{:S(2)}, u32[]{:S(2)}) collective-permute-start(bf16[72,2048]{1,0:T(8,128)(2,1)} %get-tuple-element.82), channel_id=1, source_target_pairs={{0,2},{1,3},{2,0},{3,1},{4,6},{5,7},{6,4},{7,5},{8,10},{9,11},{10,... | collective-permute-start | bytes 884744 | tf_op jit(solution)/shard_map/ppermute | solution.py:28
  69.3 15.1 %collective-permute-start.4 = (bf16[72,2048]{1,0:T(8,128)(2,1)}, bf16[72,2048]{1,0:T(8,128)(2,1)S(1)}, u32[]{:S(2)}, u32[]{:S(2)}) collective-permute-start(bf16[72,2048]{1,0:T(8,128)(2,1)} %get-tuple-element.83), channel_id=1, source_target_pairs={{0,3},{1,2},{2,1},{3,0},{4,7},{5,6},{6,5},{7,4},{8,11},{9,10},{10,... | collective-permute-start | bytes 884744 | tf_op jit(solution)/shard_map/ppermute | solution.py:28
  85.2 45.0 %all-to-all-start.3 = ((bf16[4,3,72,2048]{3,2,1,0:T(8,128)(2,1)}), bf16[4,3,72,2048]{3,2,1,0:T(8,128)(2,1)}, u32[]{:S(2)}, u32[]{:S(2)}) async-start(bf16[4,3,72,2048]{3,2,1,0:T(8,128)(2,1)} %get-tuple-element.89), calls=%async_computation.3 | async-start | bytes 7077888 | tf_op jit(solution)/shard_map/all_to_all | solution.py:594
  109.1 4.4 %collective-permute-start.6 = (bf16[4,128,2048]{2,1,0:T(8,128)(2,1)}, bf16[4,128,2048]{2,1,0:T(8,128)(2,1)S(1)}, u32[]{:S(2)}, u32[]{:S(2)}) collective-permute-start(bf16[4,128,2048]{2,1,0:T(8,128)(2,1)} %bitcast.79), channel_id=1, source_target_pairs={{0,4},{4,0},{1,5},{5,1},{2,6},{6,2},{3,7},{7,3},{8,12},{12,8},{9,1... | collective-permute-start | bytes 6291464 | tf_op jit(solution)/shard_map/ppermute | solution.py:28
  130.3 18.0 %all-to-all-start.2 = ((bf16[4,72,2048]{2,1,0:T(8,128)(2,1)}), bf16[4,72,2048]{2,1,0:T(8,128)(2,1)S(1)}, u32[]{:S(2)}, u32[]{:S(2)}) async-start(bf16[4,72,2048]{2,1,0:T(8,128)(2,1)} %select_scaled.5.refs_0_), calls=%async_computation.2 | async-start | bytes 2359296 | tf_op jit(solution)/shard_map/all_to_all | solution.py:594
  149.3 18.0 %all-to-all-start.4 = ((bf16[4,72,2048]{2,1,0:T(8,128)(2,1)}), bf16[4,72,2048]{2,1,0:T(8,128)(2,1)S(1)}, u32[]{:S(2)}, u32[]{:S(2)}) async-start(bf16[4,72,2048]{2,1,0:T(8,128)(2,1)} %select_scaled.6.refs_4_), calls=%async_computation.4 | async-start | bytes 2359296 | tf_op jit(solution)/shard_map/all_to_all | solution.py:594
  167.3 24.3 %all-to-all-start.5 = ((bf16[4,72,2048]{2,1,0:T(8,128)(2,1)}), bf16[4,72,2048]{2,1,0:T(8,128)(2,1)}, u32[]{:S(2)}, u32[]{:S(2)}) async-start(bf16[4,72,2048]{2,1,0:T(8,128)(2,1)} %select_scaled.7.refs_4_), calls=%async_computation.5 | async-start | bytes 2359296 | tf_op jit(solution)/shard_map/all_to_all | solution.py:594
  171.6 23.8 %collective-permute-start.10 = (bf16[72,2048]{1,0:T(8,128)(2,1)}, bf16[72,2048]{1,0:T(8,128)(2,1)}, u32[]{:S(2)}, u32[]{:S(2)}) collective-permute-start(bf16[72,2048]{1,0:T(8,128)(2,1)} %get-tuple-element.102), channel_id=1, source_target_pairs={{0,3},{1,2},{2,1},{3,0},{4,7},{5,6},{6,5},{7,4},{8,11},{9,10},{10,... | collective-permute-start | bytes 884744 | tf_op jit(solution)/shard_map/ppermute | solution.py:28
  174.4 24.4 %collective-permute-start.8 = (bf16[72,2048]{1,0:T(8,128)(2,1)}, bf16[72,2048]{1,0:T(8,128)(2,1)}, u32[]{:S(2)}, u32[]{:S(2)}) collective-permute-start(bf16[72,2048]{1,0:T(8,128)(2,1)} %get-tuple-element.100), channel_id=1, source_target_pairs={{0,1},{1,0},{2,3},{3,2},{4,5},{5,4},{6,7},{7,6},{8,9},{9,8},{10,11... | collective-permute-start | bytes 884744 | tf_op jit(solution)/shard_map/ppermute | solution.py:28
  175.0 23.8 %collective-permute-start.9 = (bf16[72,2048]{1,0:T(8,128)(2,1)}, bf16[72,2048]{1,0:T(8,128)(2,1)}, u32[]{:S(2)}, u32[]{:S(2)}) collective-permute-start(bf16[72,2048]{1,0:T(8,128)(2,1)} %get-tuple-element.101), channel_id=1, source_target_pairs={{0,2},{1,3},{2,0},{3,1},{4,6},{5,7},{6,4},{7,5},{8,10},{9,11},{10,... | collective-permute-start | bytes 884744 | tf_op jit(solution)/shard_map/ppermute | solution.py:28
  203.7 1.6 collective-permute-start.16
  205.4 8.4 %collective-permute-start.17 = (bf16[128,1024]{1,0:T(8,128)(2,1)S(1)}, bf16[128,1024]{1,0:T(8,128)(2,1)S(1)}, u32[]{:S(2)}, u32[]{:S(2)}) collective-permute-start(bf16[128,1024]{1,0:T(8,128)(2,1)S(1)} %add_convert_fusion.6), channel_id=1, source_target_pairs={{0,8},{8,0},{16,24},{24,16},{1,9},{9,1},{17,25},{25,17},{2,10},{10... | collective-permute-start | bytes 786440 | tf_op jit(solution)/shard_map/ppermute | solution.py:28
  206.9 20.7 %collective-permute-start.13 = (bf16[72,2048]{1,0:T(8,128)(2,1)S(1)}, bf16[72,2048]{1,0:T(8,128)(2,1)}, u32[]{:S(2)}, u32[]{:S(2)}) collective-permute-start(bf16[72,2048]{1,0:T(8,128)(2,1)S(1)} %copy-done.28), channel_id=1, source_target_pairs={{0,1},{1,0},{2,3},{3,2},{4,5},{5,4},{6,7},{7,6},{8,9},{9,8},{10,11... | collective-permute-start | bytes 884744 | tf_op jit(solution)/shard_map/ppermute | solution.py:28
  208.3 20.0 %collective-permute-start.14 = (bf16[72,2048]{1,0:T(8,128)(2,1)S(1)}, bf16[72,2048]{1,0:T(8,128)(2,1)}, u32[]{:S(2)}, u32[]{:S(2)}) collective-permute-start(bf16[72,2048]{1,0:T(8,128)(2,1)S(1)} %copy-done.27), channel_id=1, source_target_pairs={{0,2},{1,3},{2,0},{3,1},{4,6},{5,7},{6,4},{7,5},{8,10},{9,11},{10,... | collective-permute-start | bytes 884744 | tf_op jit(solution)/shard_map/ppermute | solution.py:28
  208.9 20.9 %collective-permute-start.15 = (bf16[72,2048]{1,0:T(8,128)(2,1)}, bf16[72,2048]{1,0:T(8,128)(2,1)}, u32[]{:S(2)}, u32[]{:S(2)}) collective-permute-start(bf16[72,2048]{1,0:T(8,128)(2,1)} %get-tuple-element.113), channel_id=1, source_target_pairs={{0,3},{1,2},{2,1},{3,0},{4,7},{5,6},{6,5},{7,4},{8,11},{9,10},{10,... | collective-permute-start | bytes 884744 | tf_op jit(solution)/shard_map/ppermute | solution.py:28
  213.9 27.4 %collective-permute-start.24 = (bf16[128,1024]{1,0:T(8,128)(2,1)S(1)}, bf16[128,1024]{1,0:T(8,128)(2,1)}, u32[]{:S(2)}, u32[]{:S(2)}) collective-permute-start(bf16[128,1024]{1,0:T(8,128)(2,1)S(1)} %add_convert_fusion.5), channel_id=1, source_target_pairs={{0,16},{8,24},{16,0},{24,8},{1,17},{9,25},{17,1},{25,9},{2,18},{10... | collective-permute-start | bytes 786440 | tf_op jit(solution)/shard_map/ppermute | solution.py:28
  226.3 16.7 %collective-permute-start.21 = (bf16[72,2048]{1,0:T(8,128)(2,1)}, bf16[72,2048]{1,0:T(8,128)(2,1)}, u32[]{:S(2)}, u32[]{:S(2)}) collective-permute-start(bf16[72,2048]{1,0:T(8,128)(2,1)} %get-tuple-element.123), channel_id=1, source_target_pairs={{0,1},{1,0},{2,3},{3,2},{4,5},{5,4},{6,7},{7,6},{8,9},{9,8},{10,11... | collective-permute-start | bytes 884744 | tf_op jit(solution)/shard_map/ppermute | solution.py:28
  227.7 15.4 %collective-permute-start.22 = (bf16[72,2048]{1,0:T(8,128)(2,1)}, bf16[72,2048]{1,0:T(8,128)(2,1)}, u32[]{:S(2)}, u32[]{:S(2)}) collective-permute-start(bf16[72,2048]{1,0:T(8,128)(2,1)} %get-tuple-element.124), channel_id=1, source_target_pairs={{0,2},{1,3},{2,0},{3,1},{4,6},{5,7},{6,4},{7,5},{8,10},{9,11},{10,... | collective-permute-start | bytes 884744 | tf_op jit(solution)/shard_map/ppermute | solution.py:28
  228.3 14.8 %collective-permute-start.23 = (bf16[72,2048]{1,0:T(8,128)(2,1)}, bf16[72,2048]{1,0:T(8,128)(2,1)}, u32[]{:S(2)}, u32[]{:S(2)}) collective-permute-start(bf16[72,2048]{1,0:T(8,128)(2,1)} %get-tuple-element.125), channel_id=1, source_target_pairs={{0,3},{1,2},{2,1},{3,0},{4,7},{5,6},{6,5},{7,4},{8,11},{9,10},{10,... | collective-permute-start | bytes 884744 | tf_op jit(solution)/shard_map/ppermute | solution.py:28
  229.8 33.3 %collective-permute-start.11 = (bf16[128,2048]{1,0:T(8,128)(2,1)}, bf16[128,2048]{1,0:T(8,128)(2,1)}, u32[]{:S(2)}, u32[]{:S(2)}) collective-permute-start(bf16[128,2048]{1,0:T(8,128)(2,1)} %get-tuple-element.110), channel_id=1, source_target_pairs={{0,4},{4,0},{1,5},{5,1},{2,6},{6,2},{3,7},{7,3},{8,12},{12,8},{9,1... | collective-permute-start | bytes 1572872 | tf_op jit(solution)/shard_map/ppermute | solution.py:28
  242.3 4.4 %collective-permute-start.27 = (bf16[128,1024]{1,0:T(8,128)(2,1)S(1)}, bf16[128,1024]{1,0:T(8,128)(2,1)S(1)}, u32[]{:S(2)}, u32[]{:S(2)}) collective-permute-start(bf16[128,1024]{1,0:T(8,128)(2,1)S(1)} %fusion.12), channel_id=1, source_target_pairs={{3,2},{7,6},{11,10},{15,14},{19,18},{23,22},{27,26},{31,30}} | collective-permute-start | bytes 786440 | tf_op jit(solution)/shard_map/ppermute | solution.py:724
  246.2 16.9 %collective-permute-start.25 = (bf16[128,2048]{1,0:T(8,128)(2,1)}, bf16[128,2048]{1,0:T(8,128)(2,1)}, u32[]{:S(2)}, u32[]{:S(2)}) collective-permute-start(bf16[128,2048]{1,0:T(8,128)(2,1)} %get-tuple-element.131), channel_id=1, source_target_pairs={{0,4},{4,0},{1,5},{5,1},{2,6},{6,2},{3,7},{7,3},{8,12},{12,8},{9,1... | collective-permute-start | bytes 1572872 | tf_op jit(solution)/shard_map/ppermute | solution.py:28
  246.8 15.2 %collective-permute-start.28 = (bf16[128,1024]{1,0:T(8,128)(2,1)S(1)}, bf16[128,1024]{1,0:T(8,128)(2,1)}, u32[]{:S(2)}, u32[]{:S(2)}) collective-permute-start(bf16[128,1024]{1,0:T(8,128)(2,1)S(1)} %add.151), channel_id=1, source_target_pairs={{3,1},{2,0},{7,5},{6,4},{11,9},{10,8},{15,13},{14,12},{19,17},{18,... | collective-permute-start | bytes 786440 | tf_op jit(solution)/shard_map/ppermute | solution.py:724
  250.8 15.5 %collective-permute-start.18 = (bf16[128,2048]{1,0:T(8,128)(2,1)}, bf16[128,2048]{1,0:T(8,128)(2,1)S(1)}, u32[]{:S(2)}, u32[]{:S(2)}) collective-permute-start(bf16[128,2048]{1,0:T(8,128)(2,1)} %get-tuple-element.122), channel_id=1, source_target_pairs={{0,4},{4,0},{1,5},{5,1},{2,6},{6,2},{3,7},{7,3},{8,12},{12,8},{9,1... | collective-permute-start | bytes 1572872 | tf_op jit(solution)/shard_map/ppermute | solution.py:28
  263.1 7.4 %collective-permute-start.29 = (bf16[128,1024]{1,0:T(8,128)(2,1)S(1)}, bf16[128,1024]{1,0:T(8,128)(2,1)S(1)}, u32[]{:S(2)}, u32[]{:S(2)}) collective-permute-start(bf16[128,1024]{1,0:T(8,128)(2,1)S(1)} %add.152), channel_id=1, source_target_pairs={{0,4},{4,0},{1,5},{5,1},{2,6},{6,2},{3,7},{7,3},{8,12},{12,8},{9,1... | collective-permute-start | bytes 786440 | tf_op jit(solution)/shard_map/ppermute | solution.py:28
  268.8 28.1 %collective-permute-start.19 = (bf16[128,2048]{1,0:T(8,128)(2,1)}, bf16[128,2048]{1,0:T(8,128)(2,1)}, u32[]{:S(2)}, u32[]{:S(2)}) collective-permute-start(bf16[128,2048]{1,0:T(8,128)(2,1)} %get-tuple-element.165), channel_id=1, source_target_pairs={{8,24},{24,8},{9,25},{25,9},{10,26},{26,10},{11,27},{27,11},{12,28... | collective-permute-start | bytes 1572872 | tf_op jit(solution)/shard_map/ppermute | solution.py:656
  274.1 21.4 %collective-permute-start.30 = (bf16[1024,128]{1,0:T(8,128)(2,1)}, bf16[1024,128]{1,0:T(8,128)(2,1)}, u32[]{:S(2)}, u32[]{:S(2)}) collective-permute-start(bf16[1024,128]{1,0:T(8,128)(2,1)} %get-tuple-element.172), channel_id=1, source_target_pairs={{0,4},{4,0},{1,5},{5,1},{2,6},{6,2},{3,7},{7,3},{8,12},{12,8},{9,1... | collective-permute-start | bytes 786440 | tf_op jit(solution)/shard_map/ppermute | solution.py:28
  275.8 11.6 %collective-permute-start.32 = (f32[32,512]{1,0:T(8,128)}, f32[32,512]{1,0:T(8,128)}, u32[]{:S(2)}, u32[]{:S(2)}) collective-permute-start(f32[32,512]{1,0:T(8,128)} %get-tuple-element.169), channel_id=1, source_target_pairs={{0,1},{1,0},{2,3},{3,2},{4,5},{5,4},{6,7},{7,6},{8,9},{9,8},{10,11... | collective-permute-start | bytes 196616 | tf_op jit(solution)/shard_map/ppermute | solution.py:28
  275.8 11.6 %collective-permute-start.33 = (f32[32,512]{1,0:T(8,128)}, f32[32,512]{1,0:T(8,128)}, u32[]{:S(2)}, u32[]{:S(2)}) collective-permute-start(f32[32,512]{1,0:T(8,128)} %get-tuple-element.171), channel_id=1, source_target_pairs={{0,2},{1,3},{2,0},{3,1},{4,6},{5,7},{6,4},{7,5},{8,10},{9,11},{10,... | collective-permute-start | bytes 196616 | tf_op jit(solution)/shard_map/ppermute | solution.py:28
  275.8 17.8 %collective-permute-start.34 = (f32[32,512]{1,0:T(8,128)}, f32[32,512]{1,0:T(8,128)}, u32[]{:S(2)}, u32[]{:S(2)}) collective-permute-start(f32[32,512]{1,0:T(8,128)} %get-tuple-element.170), channel_id=1, source_target_pairs={{0,3},{1,2},{2,1},{3,0},{4,7},{5,6},{6,5},{7,4},{8,11},{9,10},{10,... | collective-permute-start | bytes 196616 | tf_op jit(solution)/shard_map/ppermute | solution.py:28
  279.2 23.0 %copy-start.15 = (bf16[128,1024]{1,0:T(8,128)(2,1)S(1)}, bf16[128,1024]{1,0:T(8,128)(2,1)}, u32[]{:S(2)}) copy-start(bf16[128,1024]{1,0:T(8,128)(2,1)} %copy-done.14) | copy-start | bytes 786436
  279.3 23.0 %copy-start.17 = (bf16[128,1024]{1,0:T(8,128)(2,1)S(1)}, bf16[128,1024]{1,0:T(8,128)(2,1)}, u32[]{:S(2)}) copy-start(bf16[128,1024]{1,0:T(8,128)(2,1)} %copy-done.16) | copy-start | bytes 786436
  287.4 41.5 %collective-permute-start.7 = (bf16[128,2048]{1,0:T(8,128)(2,1)}, bf16[128,2048]{1,0:T(8,128)(2,1)}, u32[]{:S(2)}, u32[]{:S(2)}) collective-permute-start(bf16[128,2048]{1,0:T(8,128)(2,1)} %get-tuple-element.99), channel_id=1, source_target_pairs={{0,4},{4,0},{1,5},{5,1},{2,6},{6,2},{3,7},{7,3},{8,12},{12,8},{9,1... | collective-permute-start | bytes 1572872 | tf_op jit(solution)/shard_map/ppermute | solution.py:28
  287.4 31.0 %collective-permute-start.12 = (bf16[128,2048]{1,0:T(8,128)(2,1)}, bf16[128,2048]{1,0:T(8,128)(2,1)}, u32[]{:S(2)}, u32[]{:S(2)}) collective-permute-start(bf16[128,2048]{1,0:T(8,128)(2,1)} %get-tuple-element.163), channel_id=1, source_target_pairs={{0,24},{24,0},{1,25},{25,1},{2,26},{26,2},{3,27},{27,3},{4,28},{28... | collective-permute-start | bytes 1572872 | tf_op jit(solution)/shard_map/ppermute | solution.py:656
  293.6 24.2 %collective-permute-start.20 = (bf16[128,2048]{1,0:T(8,128)(2,1)}, bf16[128,2048]{1,0:T(8,128)(2,1)}, u32[]{:S(2)}, u32[]{:S(2)}) collective-permute-start(bf16[128,2048]{1,0:T(8,128)(2,1)} %get-tuple-element.166), channel_id=1, source_target_pairs={{0,8},{8,16},{16,0},{1,9},{9,17},{17,1},{2,10},{10,18},{18,2},{3,1... | collective-permute-start | bytes 1572872 | tf_op jit(solution)/shard_map/ppermute | solution.py:656
  295.5 31.1 %collective-permute-start.26 = (bf16[128,2048]{1,0:T(8,128)(2,1)}, bf16[128,2048]{1,0:T(8,128)(2,1)}, u32[]{:S(2)}, u32[]{:S(2)}) collective-permute-start(bf16[128,2048]{1,0:T(8,128)(2,1)} %get-tuple-element.162), channel_id=1, source_target_pairs={{16,24},{24,16},{17,25},{25,17},{18,26},{26,18},{19,27},{27,19},{2... | collective-permute-start | bytes 1572872 | tf_op jit(solution)/shard_map/ppermute | solution.py:656
  297.0 31.9 %collective-permute-start.31 = (bf16[128,2048]{1,0:T(8,128)(2,1)}, bf16[128,2048]{1,0:T(8,128)(2,1)}, u32[]{:S(2)}, u32[]{:S(2)}) collective-permute-start(bf16[128,2048]{1,0:T(8,128)(2,1)} %get-tuple-element.164), channel_id=1, source_target_pairs={{0,16},{8,0},{16,8},{1,17},{9,1},{17,9},{2,18},{10,2},{18,10},{3,1... | collective-permute-start | bytes 1572872 | tf_op jit(solution)/shard_map/ppermute | solution.py:656
  317.8 14.4 %collective-permute-start.35 = (bf16[1024,128]{1,0:T(8,128)(2,1)S(1)}, bf16[1024,128]{1,0:T(8,128)(2,1)S(1)}, u32[]{:S(2)}, u32[]{:S(2)}) collective-permute-start(bf16[1024,128]{1,0:T(8,128)(2,1)S(1)} %add_convert_fusion.3), channel_id=1, source_target_pairs={{0,0},{4,16},{8,4},{12,20},{16,8},{20,24},{24,12},{28,28},{1,1},{5... | collective-permute-start | bytes 786440 | tf_op jit(solution)/shard_map/ppermute | solution.py:804
  (27 other events, 138.4 us)
Sparse Core Ops, SparseCore 0:
  9.6 53.1 all-gather.6
  64.4 44.6 all-gather.4
where the time goes:
time: 342 us; the launch traced here: 340 us
  Pallas kernels  121 us (35%)
  waiting for transfers between devices  101 us (30%)
  starting transfers between devices  67.6 us (20%)
  other arithmetic  17.1 us (5%)
  between operations  14.7 us (4%)
  local copies, waits for them, and re-layouts  12.3 us (4%)
  matrix products  6.66 us (2%)
    pallas_call x4, Pallas kernels, expert(): pl.pallas_call(functools.partial(expert_kernel, n_key), grid=(steps,), ou...  40.1 us
    all_to_all x6, waiting for transfers between devices, exchange(): return lax.all_to_all(x, 'key', split_axis=0, concat_axis=0, tiled=True)  33.7 us
    all_to_all x6, starting transfers between devices, exchange(): return lax.all_to_all(x, 'key', split_axis=0, concat_axis=0, tiled=True)  24.9 us
    pallas_call x3, Pallas kernels, weight_grad(): pl.pallas_call(weights_kernel, grid=(height // tile,), out_shape=[jax.Sha...  24.5 us
    ppermute x28, waiting for transfers between devices, swap(): return lax.ppermute(block, axis, [(i, i ^ mask) for i in range(count)])  24.2 us
    ppermute x28, starting transfers between devices, swap(): return lax.ppermute(block, axis, [(i, i ^ mask) for i in range(count)])  23.4 us
    all_gather x1, waiting for transfers between devices, layer(): column_up = lax.all_gather(upstream, 'z')  19.1 us
    ppermute x5, starting transfers between devices, pass_z(): return lax.ppermute(block, 'z', route)  16.4 us
  transfers between devices with their start and end apart: 44, of which 19 were waited for; matrix products, arithmetic and copies ran while one was open for 8% of the time, Pallas kernels for 34%

commit v1 on v0

--- a/solution.py
+++ b/solution.py
@@ -209,7 +209,7 @@
     )
     grad_down = dot(hidden, scaled_in, ((0,), (0,))).astype(BF)
     grad_gate_up = dot(expert_in, d_gate_up, ((0,), (0,))).astype(BF)
-    return (d_resid, grad_gate_up, grad_down, *attend(last_to_all(d_resid))[0])
+    return (d_resid, grad_gate_up, grad_down, *attend(last_to_all(d_resid), lambda x: x)[0])
 
 
 INFO_ROWS = 16
@@ -649,11 +649,7 @@
 
     def run_total(m):
         keep, send = parts[m]
-        totals[m] = keep + swap(send, "core", 1).astype(F32)
-        totals[m] = totals[m] if m == 0 else totals[m].astype(BF)
-
-    def pass_z(block, route):
-        return lax.ppermute(block, "z", route)
+        totals[m] = (keep + swap(send, "core", 1).astype(F32)).astype(BF)
 
     def then(*others):
         state["after"] = after(state["after"], *others)
@@ -683,7 +679,8 @@
     fetch_scaled(3)
     run_combine(0)
     run_expert(2, scaled[2], gate, up)
-    then(scaled[3])
+    run_expert(3, scaled[3], gate, up)
+    run_combine(2)
     run_combine(1)
 
     last = z == n_z - 1
@@ -699,45 +696,49 @@
     held = held.astype(BF)
     run_total(0)
     run_total(1)
-    arrived_a = pass_z(totals[1], [(0, 3), (3, 0)])
-    then(held)
-    run_expert(3, scaled[3], gate, up)
+    run_total(2)
+    scaled, hidden, d_gate, d_up = kept
+    grad_down, state["after"] = weight_grad(hidden, scaled, 384, state["after"])
     held = (held.astype(F32) + swap(held, "z", 1).astype(F32)).astype(BF)
     then(held)
-    run_combine(2)
-    run_total(2)
-    arrived_b = pass_z(jnp.where(last, totals[2], totals[1]), [(1, 3), (3, 1)])
-    arrived_d = pass_z(totals[2], [(0, 1), (1, 2), (2, 0)])
-    held = (held.astype(F32) + swap(held, "z", 2).astype(F32)).astype(BF)
+    run_combine(3)
+    arrived = swap(held, "z", 2)
+    held = (held.astype(F32) + arrived.astype(F32)).astype(BF)
     held = jnp.where(key == n_key - 1, held, jnp.zeros_like(held))
-    scaled, hidden, d_gate, d_up = kept
-    grad_down, state["after"] = weight_grad(hidden, scaled, 384, state["after"])
+    run_total(3)
+    by_height = [
+        pick(z, [totals[0 if at == to else ORDER[at].index(to) + 1] for at in range(n_z)])
+        for to in range(n_z)
+    ]
+    summed = lax.psum_scatter(
+        after(jnp.concatenate(by_height, axis=0), arrived),
+        "z",
+        scatter_dimension=0,
+        tiled=True,
+    )
     then(held)
-    run_combine(3)
-    run_total(3)
-    arrived_c = pass_z(jnp.where(last, totals[3], totals[1]), [(2, 3), (3, 2)])
-    arrived_e = pass_z(totals[3], [(0, 2), (1, 0), (2, 1)])
+    work = [(d_gate, 0), (d_up, 1)]
+    grads = None
     sources = [n_key - 1]
     bit = 1
     while bit < n_key:
         route = [(i, i ^ bit) for i in sources]
-        held = held + lax.ppermute(held, "key", route)
+        arrived = lax.ppermute(held, "key", route)
+        if work:
+            right, part = work.pop(0)
+            grads, state["after"] = weight_grad(ins, right, 512, state["after"], part, 2, grads)
+        held = held + after(arrived, state["after"])
+        then(held)
         sources += [target for _, target in route]
         bit *= 2
-    then(held)
-    grads, state["after"] = weight_grad(ins, d_gate, 512, state["after"], 0, 2)
+    for right, part in work:
+        grads, state["after"] = weight_grad(ins, right, 512, state["after"], part, 2, grads)
     other = swap(held, "core", 1)
     window = jnp.concatenate(
         [jnp.where(first, held, other), jnp.where(first, other, held)], axis=1
     )
-    outs, done = attend(window)
-    then(arrived_a, arrived_b, arrived_d, *done)
-    grads, state["after"] = weight_grad(ins, d_up, 512, state["after"], 1, 2, grads)
-    resid = upstream.astype(F32) + totals[0]
-    for arrived in (arrived_a, arrived_b, arrived_d):
-        resid = resid + arrived.astype(F32)
-    for arrived in (arrived_c, arrived_e):
-        resid = resid + after(arrived, state["after"]).astype(F32)
+    outs, done = attend(after(window, state["after"]), lambda x: x)
+    resid = upstream.astype(F32) + after(summed, *done).astype(F32)
     return (resid.astype(BF), grads, grad_down, *outs)
 
 
@@ -783,7 +784,7 @@
     scores = dot(query_rows, key_head, ((1,), (1,))) * score_scale
     probs = jnp.where(visible, jnp.exp(scores - attn_lse.reshape(-1)[:, None]), 0.0)
 
-    def attend(window):
+    def attend(window, halfway):
         d_attn = dot(window, w_out, ((1,), (1,))).astype(BF)
         column_width = d_model // n_key
         columns = lax.dynamic_slice_in_dim(window, key * column_width, column_width, 1)
@@ -791,7 +792,7 @@
         grad_rows = by_head(d_attn)
         delta = jnp.sum(grad_rows.astype(F32) * out_rows.astype(F32), axis=1)
         d_probs = dot(grad_rows, value_head, ((1,), (1,)))
-        d_scores = (probs * (d_probs - delta[:, None])).astype(BF)
+        d_scores = halfway((probs * (d_probs - delta[:, None])).astype(BF))
         d_query = dot(d_scores, key_head, ((1,), (0,))) * score_scale
         d_key = dot(d_scores, query_rows, ((0,), (0,))) * score_scale
         d_value = dot(probs.astype(BF), grad_rows, ((0,), (0,)))

time: 342 us -> 316 us (0.924)
  waiting for transfers between devices: 101 us -> 88.2 us
  starting transfers between devices: 67.6 us -> 56 us
    ppermute x7 -> x2, starting transfers between devices: 18.6 us -> 1.97 us  [layer(): arrived = lax.ppermute(held, 'key', route)]
    ppermute x7 -> x2, waiting for transfers between devices: 23 us -> 8.79 us  [layer(): arrived = lax.ppermute(held, 'key', route)]
    ppermute x28, waiting for transfers between devices: 24.2 us -> 29.2 us  [swap(): return lax.ppermute(block, axis, [(i, i ^ mask) for i in range(count)])]
    all_to_all x6, waiting for transfers between devices: 33.7 us -> 30.3 us  [exchange(): return lax.all_to_all(x, 'key', split_axis=0, concat_axis=0, tiled=True)]
    unnamed x66 -> x60, local copies, waits for them, and re-layouts: 9.73 us -> 12.4 us
  transfers between devices with their start and end apart: 44 -> 40, of which waited for: 19 -> 18; matrix products, arithmetic and copies ran while one was open for 8% -> 6% of each run, Pallas kernels for 34% -> 37%
where the time goes in v1:
time: 316 us; the launch traced here: 313 us
  Pallas kernels  121 us (38%)
  waiting for transfers between devices  88.2 us (28%)
  starting transfers between devices  56 us (18%)
  other arithmetic  14.8 us (5%)
  between operations  14.3 us (5%)
  local copies, waits for them, and re-layouts  13.4 us (4%)
  matrix products  4.86 us (2%)
    pallas_call x4, Pallas kernels, expert(): pl.pallas_call(functools.partial(expert_kernel, n_key), grid=(steps,), ou...  40.1 us
    all_to_all x6, waiting for transfers between devices, exchange(): return lax.all_to_all(x, 'key', split_axis=0, concat_axis=0, tiled=True)  30.3 us
    ppermute x28, waiting for transfers between devices, swap(): return lax.ppermute(block, axis, [(i, i ^ mask) for i in range(count)])  29.2 us
    ppermute x28, starting transfers between devices, swap(): return lax.ppermute(block, axis, [(i, i ^ mask) for i in range(count)])  26.3 us
    pallas_call x3, Pallas kernels, weight_grad(): pl.pallas_call(weights_kernel, grid=(height // tile,), out_shape=[jax.Sha...  24.7 us
    all_to_all x6, starting transfers between devices, exchange(): return lax.all_to_all(x, 'key', split_axis=0, concat_axis=0, tiled=True)  24.1 us
    all_gather x1, waiting for transfers between devices, layer(): column_up = lax.all_gather(upstream, 'z')  19.2 us
    pallas_call x2, Pallas kernels, gate_up(): pl.pallas_call(functools.partial(gate_kernel, n_key, count), grid=(steps,...  16.4 us
  transfers between devices with their start and end apart: 40, of which 18 were waited for; matrix products, arithmetic and copies ran while one was open for 6% of the time, Pallas kernels for 37%

profile of v1, /device:TPU:0, one launch (start us, length us, event | category | flops | bytes accessed | tf_op | source)
XLA Modules:
  0.0 312.6 jit_solution(11039447860474548712)
XLA Ops:
  7.2 2.1 build_block.1.after
  12.5 3.7 %select_inputs.2 = (bf16[4,1,72,2048]{3,2,1,0:T(8,128)(2,1)}, bf16[1,288,256]{2,1,0:T(8,128)(2,1)}, f32[1,288,128]{2,1,0:T(8,128)}) custom-call(s32[2]{0:T(128)} %pad_add_fusion.meta, bf16[1,144,2048]{2,1,0:T(8,128)(2,1)} %bitcast.84, bf16[1,144,2048]{2,1,0:T(8,128)(2,1)} %bitcast.91, bf16[1,144,2048]{2,1,0:T(8,128)(2,1)} %bitcast.85, ...), custom_call_target="tpu_custom_call" | custom-call | flops 1000 | bytes 1000 | tf_op jit(solution)/shard_map/select_inputs/pallas_call | solution.py:304
  16.2 5.1 %all-to-all-start.1 = ((bf16[4,1,72,2048]{3,2,1,0:T(8,128)(2,1)}), bf16[4,1,72,2048]{3,2,1,0:T(8,128)(2,1)}, u32[]{:S(2)}, u32[]{:S(2)}) async-start(bf16[4,1,72,2048]{3,2,1,0:T(8,128)(2,1)} %get-tuple-element.74), calls=%async_computation.1 | async-start | bytes 2359296 | tf_op jit(solution)/shard_map/all_to_all | solution.py:594
  24.1 3.4 %select_scaled.4.refs_0_ = bf16[4,72,2048]{2,1,0:T(8,128)(2,1)} custom-call(s32[2]{0:T(128)} %pad_add_fusion.meta, bf16[1,128,2048]{2,1,0:T(8,128)(2,1)} %bitcast.89, bf16[1,128,2048]{2,1,0:T(8,128)(2,1)} %bitcast.100, bf16[1,288,256]{2,1,0:T(8,128)(2,1)} %get-tuple-element.72.hot_ref.after, f32[1,288,128]{2,1,0:T(8,128)} %get-tuple-element.73.scale_ref, ...), custom_call_target="tpu_custom_call" | custom-call | flops 1000 | bytes 1000 | tf_op jit(solution)/shard_map/select_scaled/pallas_call | solution.py:351
  27.5 9.8 %all-to-all-done.1.pieces = bf16[4,1,72,2048]{3,2,1,0:T(8,128)(2,1)} async-done(((bf16[4,1,72,2048]{3,2,1,0:T(8,128)(2,1)}), bf16[4,1,72,2048]{3,2,1,0:T(8,128)(2,1)}, u32[]{:S(2)}, u32[]{:S(2)}) %all-to-all-start.1) | async-done | bytes 1179680 | tf_op jit(solution)/shard_map/all_to_all | solution.py:594
  37.4 3.5 %all-to-all-start = ((bf16[4,72,2048]{2,1,0:T(8,128)(2,1)}), bf16[4,72,2048]{2,1,0:T(8,128)(2,1)S(1)}, u32[]{:S(2)}, u32[]{:S(2)}) async-start(bf16[4,72,2048]{2,1,0:T(8,128)(2,1)} %select_scaled.4.refs_0_), calls=%async_computation | async-start | bytes 2359296 | tf_op jit(solution)/shard_map/all_to_all | solution.py:594
  41.3 1.9 bitcast_select_fusion
  43.2 5.9 %gate_up.2 = (bf16[1152,2048]{1,0:T(8,128)(2,1)}, f32[288,768]{1,0:T(8,128)}, f32[288,768]{1,0:T(8,128)}) custom-call(bf16[4,1,72,2048]{3,2,1,0:T(8,128)(2,1)} %all-to-all-done.1.pieces, bf16[2048,1536]{1,0:T(8,128)(2,1)} %bitcast.64, bf16[2048,1536]{1,0:T(8,128)(2,1)} %bitcast.65, bf16[4,72,2048]{2,1,0:T(8,128)(2,1)} %select_scaled.4.refs_0_), custom_call_target="tpu_custom_call" | custom-call | flops 1000 | bytes 1000 | tf_op jit(solution)/shard_map/gate_up/pallas_call | solution.py:391
  49.2 6.8 %all-to-all-done.pieces = bf16[4,72,2048]{2,1,0:T(8,128)(2,1)S(1)} async-done(((bf16[4,72,2048]{2,1,0:T(8,128)(2,1)}), bf16[4,72,2048]{2,1,0:T(8,128)(2,1)S(1)}, u32[]{:S(2)}, u32[]{:S(2)}) %all-to-all-start) | async-done | bytes 1179680 | tf_op jit(solution)/shard_map/all_to_all | solution.py:594
  57.0 10.2 %expert_chunk.4 = (bf16[72,2048]{1,0:T(8,128)(2,1)}, bf16[72,2048]{1,0:T(8,128)(2,1)}, bf16[72,2048]{1,0:T(8,128)(2,1)}, bf16[72,2048]{1,0:T(8,128)(2,1)}, bf16[...) custom-call(s32[1]{0:T(128)} %bitcast.meta, ...), custom_call_target="tpu_custom_call" | custom-call | flops 1000 | bytes 1000 | tf_op jit(solution)/shard_map/expert_chunk/pallas_call | solution.py:461
  72.1 7.7 %select_inputs.3 = (bf16[4,3,72,2048]{3,2,1,0:T(8,128)(2,1)}, bf16[3,288,256]{2,1,0:T(8,128)(2,1)}, f32[3,288,128]{2,1,0:T(8,128)}) custom-call(s32[4]{0:T(128)} %pad_add_fusion.1.meta, bf16[4,144,2048]{2,1,0:T(8,128)(2,1)} %bitcast.87, bf16[4,144,2048]{2,1,0:T(8,128)(2,1)} %collective-permute-done.5.xb.ib, bf16[4,144,2048]{2,1,0:T(8,128)(2,1)} %bitcast.88, ...), custom_call_target="tpu_custom_call" | custom-call | flops 1000 | bytes 1000 | tf_op jit(solution)/shard_map/select_inputs/pallas_call | solution.py:304
  79.8 4.5 %collective-permute-done.3.refs_2_ = bf16[72,2048]{1,0:T(8,128)(2,1)S(1)} collective-permute-done((bf16[72,2048]{1,0:T(8,128)(2,1)}, bf16[72,2048]{1,0:T(8,128)(2,1)S(1)}, u32[]{:S(2)}, u32[]{:S(2)}) %collective-permute-start.3) | collective-permute-done | bytes 294944 | tf_op jit(solution)/shard_map/ppermute | solution.py:28
  85.2 4.7 %all-to-all-start.3 = ((bf16[4,3,72,2048]{3,2,1,0:T(8,128)(2,1)}), bf16[4,3,72,2048]{3,2,1,0:T(8,128)(2,1)}, u32[]{:S(2)}, u32[]{:S(2)}) async-start(bf16[4,3,72,2048]{3,2,1,0:T(8,128)(2,1)} %get-tuple-element.86), calls=%async_computation.3 | async-start | bytes 7077888 | tf_op jit(solution)/shard_map/all_to_all | solution.py:594
  89.9 19.2 %all-gather.5.cloned.1.call-done = bf16[512,2048]{1,0:T(8,128)(2,1)} async-done(((bf16[128,2048]{1,0:T(8,128)(2,1)}), bf16[512,2048]{1,0:T(8,128)(2,1)}) %all-gather.5.cloned.1.call-update) | async-done | bytes 2097168 | tf_op jit(solution)/shard_map/all_gather | solution.py:586
  109.2 4.4 %collective-permute-done.6.xb = bf16[4,128,2048]{2,1,0:T(8,128)(2,1)S(1)} collective-permute-done((bf16[4,128,2048]{2,1,0:T(8,128)(2,1)}, bf16[4,128,2048]{2,1,0:T(8,128)(2,1)S(1)}, u32[]{:S(2)}, u32[]{:S(2)}) %collective-permute-start.6) | collective-permute-done | bytes 2097184 | tf_op jit(solution)/shard_map/ppermute | solution.py:28
  114.8 3.3 %select_scaled.5.refs_0_ = bf16[4,72,2048]{2,1,0:T(8,128)(2,1)} custom-call(s32[4]{0:T(128)} %pad_add_fusion.1.meta, bf16[4,128,2048]{2,1,0:T(8,128)(2,1)} %bitcast.81, bf16[4,128,2048]{2,1,0:T(8,128)(2,1)} %copy-done.1, bf16[3,288,256]{2,1,0:T(8,128)(2,1)} %get-tuple-element.82.hot_ref.after, f32[3,288,128]{2,1,0:T(8,128)} %get-tuple-element.84.scale_ref, ...), custom_call_target="tpu_custom_call" | custom-call | flops 1000 | bytes 1000 | tf_op jit(solution)/shard_map/select_scaled/pallas_call | solution.py:351
  118.2 12.0 %all-to-all-done.3.pieces = bf16[4,3,72,2048]{3,2,1,0:T(8,128)(2,1)} async-done(((bf16[4,3,72,2048]{3,2,1,0:T(8,128)(2,1)}), bf16[4,3,72,2048]{3,2,1,0:T(8,128)(2,1)}, u32[]{:S(2)}, u32[]{:S(2)}) %all-to-all-start.3) | async-done | bytes 3538976 | tf_op jit(solution)/shard_map/all_to_all | solution.py:594
  130.2 3.5 %all-to-all-start.2 = ((bf16[4,72,2048]{2,1,0:T(8,128)(2,1)}), bf16[4,72,2048]{2,1,0:T(8,128)(2,1)S(1)}, u32[]{:S(2)}, u32[]{:S(2)}) async-start(bf16[4,72,2048]{2,1,0:T(8,128)(2,1)} %select_scaled.5.refs_0_), calls=%async_computation.2 | async-start | bytes 2359296 | tf_op jit(solution)/shard_map/all_to_all | solution.py:594
  133.8 10.5 %gate_up.3 = (bf16[1152,2048]{1,0:T(8,128)(2,1)}, f32[864,768]{1,0:T(8,128)}, f32[864,768]{1,0:T(8,128)}) custom-call(bf16[4,3,72,2048]{3,2,1,0:T(8,128)(2,1)} %all-to-all-done.3.pieces, bf16[2048,1536]{1,0:T(8,128)(2,1)} %bitcast.68, bf16[2048,1536]{1,0:T(8,128)(2,1)} %bitcast.69, ...), custom_call_target="tpu_custom_call", output_to_operand_aliasing={{0}: (4, {})} | custom-call | flops 1000 | bytes 1000 | tf_op jit(solution)/shard_map/gate_up/pallas_call | solution.py:391
  144.2 3.3 %select_scaled.6.refs_4_ = bf16[4,72,2048]{2,1,0:T(8,128)(2,1)} custom-call(s32[4]{0:T(128)} %pad_add_fusion.1.meta, bf16[4,128,2048]{2,1,0:T(8,128)(2,1)} %bitcast.82, bf16[4,128,2048]{2,1,0:T(8,128)(2,1)} %copy-done.1, bf16[3,288,256]{2,1,0:T(8,128)(2,1)} %get-tuple-element.82.hot_ref.after, f32[3,288,128]{2,1,0:T(8,128)} %get-tuple-element.84.scale_ref, ...), custom_call_target="tpu_custom_call" | custom-call | flops 1000 | bytes 1000 | tf_op jit(solution)/shard_map/select_scaled/pallas_call | solution.py:351
  149.3 3.7 %all-to-all-start.5 = ((bf16[4,72,2048]{2,1,0:T(8,128)(2,1)}), bf16[4,72,2048]{2,1,0:T(8,128)(2,1)S(1)}, u32[]{:S(2)}, u32[]{:S(2)}) async-start(bf16[4,72,2048]{2,1,0:T(8,128)(2,1)} %select_scaled.6.refs_4_), calls=%async_computation.5 | async-start | bytes 2359296 | tf_op jit(solution)/shard_map/all_to_all | solution.py:594
  153.0 10.0 %expert_chunk.5 = (bf16[72,2048]{1,0:T(8,128)(2,1)}, bf16[72,2048]{1,0:T(8,128)(2,1)}, bf16[72,2048]{1,0:T(8,128)(2,1)}, bf16[72,2048]{1,0:T(8,128)(2,1)}, bf16[...) custom-call(s32[1]{0:T(128)} %bitcast.meta, ...), custom_call_target="tpu_custom_call", output_to_operand_aliasing={{4}: (7, {}), {5}: (8, {}), {6}: (9, {}), {7}: (10, {})} | custom-call | flops 1000 | bytes 1000 | tf_op jit(solution)/shard_map/expert_chunk/pallas_call | solution.py:461
  163.0 3.3 %select_scaled.7.refs_4_ = bf16[4,72,2048]{2,1,0:T(8,128)(2,1)} custom-call(s32[4]{0:T(128)} %pad_add_fusion.1.meta, bf16[4,128,2048]{2,1,0:T(8,128)(2,1)} %bitcast.83, bf16[4,128,2048]{2,1,0:T(8,128)(2,1)} %copy-done.1, bf16[3,288,256]{2,1,0:T(8,128)(2,1)} %get-tuple-element.82.hot_ref.after, f32[3,288,128]{2,1,0:T(8,128)} %get-tuple-element.84.scale_ref, ...), custom_call_target="tpu_custom_call" | custom-call | flops 1000 | bytes 1000 | tf_op jit(solution)/shard_map/select_scaled/pallas_call | solution.py:351
  168.3 3.5 %all-to-all-start.4 = ((bf16[4,72,2048]{2,1,0:T(8,128)(2,1)}), bf16[4,72,2048]{2,1,0:T(8,128)(2,1)S(1)}, u32[]{:S(2)}, u32[]{:S(2)}) async-start(bf16[4,72,2048]{2,1,0:T(8,128)(2,1)} %select_scaled.7.refs_4_), calls=%async_computation.4 | async-start | bytes 2359296 | tf_op jit(solution)/shard_map/all_to_all | solution.py:594
  171.9 3.2 %combine_rows.4 = (f32[128,2048]{1,0:T(8,128)}, bf16[128,2048]{1,0:T(8,128)(2,1)}) custom-call(s32[1]{0:T(128)} %bitcast.meta, bf16[1,288,256]{2,1,0:T(8,128)(2,1)} %get-tuple-element.72.hot_ref.after, bf16[72,2048]{1,0:T(8,128)(2,1)} %get-tuple-element.77.after.refs_0_, bf16[72,2048]{1,0:T(8,128)(2,1)} %copy-done.20, bf16[72,2048]{1,0:T(8,128)(2,1)} %copy-done.21, ...), custom_call_target="tpu_custom_call" | custom-call | flops 1000 | bytes 1000 | tf_op jit(solution)/shard_map/combine_rows/pallas_call | solution.py:547
  175.1 9.9 %expert_chunk.6 = (bf16[72,2048]{1,0:T(8,128)(2,1)}, bf16[72,2048]{1,0:T(8,128)(2,1)}, bf16[72,2048]{1,0:T(8,128)(2,1)}, bf16[72,2048]{1,0:T(8,128)(2,1)}, bf16[...) custom-call(s32[1]{0:T(128)} %bitcast.meta, ...), custom_call_target="tpu_custom_call", output_to_operand_aliasing={{4}: (7, {}), {5}: (8, {}), {6}: (9, {}), {7}: (10, {})} | custom-call | flops 1000 | bytes 1000 | tf_op jit(solution)/shard_map/expert_chunk/pallas_call | solution.py:461
  185.0 1.9 collective-permute-start.14
  187.1 1.9 collective-permute-start.15
  191.9 3.4 %collective-permute-done.14.refs_1_ = bf16[72,2048]{1,0:T(8,128)(2,1)} collective-permute-done((bf16[72,2048]{1,0:T(8,128)(2,1)}, bf16[72,2048]{1,0:T(8,128)(2,1)}, u32[]{:S(2)}, u32[]{:S(2)}) %collective-permute-start.14) | collective-permute-done | bytes 294944 | tf_op jit(solution)/shard_map/ppermute | solution.py:28
  195.3 2.8 collective-permute-start.13
  199.2 9.9 %expert_chunk.7 = (bf16[72,2048]{1,0:T(8,128)(2,1)}, bf16[72,2048]{1,0:T(8,128)(2,1)}, bf16[72,2048]{1,0:T(8,128)(2,1)}, bf16[72,2048]{1,0:T(8,128)(2,1)}, bf16[...) custom-call(s32[1]{0:T(128)} %bitcast.meta, ...), custom_call_target="tpu_custom_call", output_to_operand_aliasing={{4}: (7, {}), {5}: (8, {}), {6}: (9, {}), {7}: (10, {})} | custom-call | flops 1000 | bytes 1000 | tf_op jit(solution)/shard_map/expert_chunk/pallas_call | solution.py:461
  209.4 3.3 %combine_rows.5 = (f32[128,2048]{1,0:T(8,128)}, bf16[128,2048]{1,0:T(8,128)(2,1)}) custom-call(s32[1]{0:T(128)} %bitcast.meta, bf16[3,288,256]{2,1,0:T(8,128)(2,1)} %get-tuple-element.82.hot_ref.after, bf16[72,2048]{1,0:T(8,128)(2,1)} %get-tuple-element.105.refs_4_.refs_0_, bf16[72,2048]{1,0:T(8,128)(2,1)} %collective-permute-done.14.refs_1_, ...), custom_call_target="tpu_custom_call" | custom-call | flops 1000 | bytes 1000 | tf_op jit(solution)/shard_map/combine_rows/pallas_call | solution.py:547
  213.7 3.3 %combine_rows.6 = (f32[128,2048]{1,0:T(8,128)}, bf16[128,2048]{1,0:T(8,128)(2,1)}) custom-call(s32[1]{0:T(128)} %bitcast.meta, bf16[3,288,256]{2,1,0:T(8,128)(2,1)} %get-tuple-element.82.hot_ref.after, bf16[72,2048]{1,0:T(8,128)(2,1)} %get-tuple-element.94.after.refs_0_, bf16[72,2048]{1,0:T(8,128)(2,1)} %collective-permute-done.11.refs_1_, ...), custom_call_target="tpu_custom_call" | custom-call | flops 1000 | bytes 1000 | tf_op jit(solution)/shard_map/combine_rows/pallas_call | solution.py:547
  221.7 2.6 collective-permute-start.10
  225.2 8.3 %weight_gradient.3 = (bf16[768,2048]{1,0:T(8,128)(2,1)}, f32[8,128]{1,0:T(8,128)}) custom-call(bf16[1152,768]{1,0:T(8,128)(2,1)} %get-tuple-element.110.left_ref, bf16[1152,2048]{1,0:T(8,128)(2,1)} %get-tuple-element.111.right_ref, f32[128,2048]{1,0:T(8,128)} %get-tuple-element.119.refs_0_), custom_call_target="tpu_custom_call" | custom-call | flops 1000 | bytes 1000 | tf_op jit(solution)/shard_map/weight_gradient/pallas_call | solution.py:501
  235.8 2.4 collective-permute-done.8.refs_1_
  238.2 3.2 %combine_rows.7 = (f32[128,2048]{1,0:T(8,128)}, bf16[128,2048]{1,0:T(8,128)(2,1)}) custom-call(s32[1]{0:T(128)} %bitcast.meta, bf16[3,288,256]{2,1,0:T(8,128)(2,1)} %get-tuple-element.82.hot_ref.after, bf16[72,2048]{1,0:T(8,128)(2,1)} %get-tuple-element.106.refs_4_.refs_0_, bf16[72,2048]{1,0:T(8,128)(2,1)} %collective-permute-done.8.refs_1_, ...), custom_call_target="tpu_custom_call" | custom-call | flops 1000 | bytes 1000 | tf_op jit(solution)/shard_map/combine_rows/pallas_call | solution.py:547
  241.4 2.7 collective-permute-start.22
  244.1 2.3 select_select_fusion.3
  246.7 1.6 pad_maximum_fusion
  248.3 8.5 %collective-permute-done.22 = bf16[128,1024]{1,0:T(8,128)(2,1)} collective-permute-done((bf16[128,1024]{1,0:T(8,128)(2,1)S(1)}, bf16[128,1024]{1,0:T(8,128)(2,1)}, u32[]{:S(2)}, u32[]{:S(2)}) %collective-permute-start.22) | collective-permute-done | bytes 262176 | tf_op jit(solution)/shard_map/ppermute | solution.py:28
  258.5 8.2 %weight_gradient.4 = (bf16[2048,1536]{1,0:T(8,128)(2,1)}, f32[8,128]{1,0:T(8,128)}) custom-call(bf16[1152,2048]{1,0:T(8,128)(2,1)} %get-tuple-element.127.left_ref, bf16[1152,768]{1,0:T(8,128)(2,1)} %get-tuple-element.128.right_ref, f32[128,2048]{1,0:T(8,128)} %get-tuple-element.129.refs_0_), custom_call_target="tpu_custom_call" | custom-call | flops 1000 | bytes 1000 | tf_op jit(solution)/shard_map/weight_gradient/pallas_call | solution.py:501
  268.2 8.8 %collective-permute-done.24 = bf16[128,1024]{1,0:T(8,128)(2,1)S(1)} collective-permute-done((bf16[128,1024]{1,0:T(8,128)(2,1)S(1)}, bf16[128,1024]{1,0:T(8,128)(2,1)S(1)}, u32[]{:S(2)}, u32[]{:S(2)}) %collective-permute-start.24) | collective-permute-done | bytes 262176 | tf_op jit(solution)/shard_map/ppermute | solution.py:726
  277.4 8.1 %weight_gradient.5 = (bf16[2048,1536]{1,0:T(8,128)(2,1)}, f32[8,128]{1,0:T(8,128)}) custom-call(bf16[1152,2048]{1,0:T(8,128)(2,1)} %get-tuple-element.127.left_ref, bf16[1152,768]{1,0:T(8,128)(2,1)} %get-tuple-element.133.right_ref, f32[8,128]{1,0:T(8,128)} %get-tuple-element.134.refs_0_, ...), custom_call_target="tpu_custom_call", output_to_operand_aliasing={{0}: (3, {})} | custom-call | flops 1000 | bytes 1000 | tf_op jit(solution)/shard_map/weight_gradient/pallas_call | solution.py:501
  291.7 2.0 collective-permute-start.27
  295.9 3.6 %collective-permute-start.30 = (bf16[1024,128]{1,0:T(8,128)(2,1)}, bf16[1024,128]{1,0:T(8,128)(2,1)}, u32[]{:S(2)}, u32[]{:S(2)}) collective-permute-start(bf16[1024,128]{1,0:T(8,128)(2,1)} %add_convert_fusion.4), channel_id=1, source_target_pairs={{0,0},{4,16},{8,4},{12,20},{16,8},{20,24},{24,12},{28,28},{1,1},{5... | collective-permute-start | bytes 786440 | tf_op jit(solution)/shard_map/ppermute | solution.py:805
  302.4 2.0 fusion.4
  304.4 1.7 copy.71
  (149 shorter events, 46.4 us)
Async XLA Ops:
  7.2 34.2 %copy-start = (bf16[1024,1024]{1,0:T(8,128)(2,1)S(1)}, bf16[1024,1024]{1,0:T(8,128)(2,1)}, u32[]{:S(2)}) copy-start(bf16[1024,1024]{1,0:T(8,128)(2,1)} %param.20) | copy-start | bytes 6291460
  7.2 60.0 %all-gather.7.cloned.1.call-start = ((), (), s32[]{:S(2)}) async-start(), calls=%async_computation.9 | async-start | bytes 2949120 | tf_op jit(solution)/shard_map/all_gather | solution.py:585
  9.3 2.4 collective-permute-start
  16.2 21.1 %all-to-all-start.1 = ((bf16[4,1,72,2048]{3,2,1,0:T(8,128)(2,1)}), bf16[4,1,72,2048]{3,2,1,0:T(8,128)(2,1)}, u32[]{:S(2)}, u32[]{:S(2)}) async-start(bf16[4,1,72,2048]{3,2,1,0:T(8,128)(2,1)} %get-tuple-element.74), calls=%async_computation.1 | async-start | bytes 2359296 | tf_op jit(solution)/shard_map/all_to_all | solution.py:594
  21.3 87.8 %all-gather.5.cloned.1.call-start = ((), (), s32[]{:S(2)}) async-start(), calls=%async_computation.8 | async-start | bytes 2621440 | tf_op jit(solution)/shard_map/all_gather | solution.py:586
  21.3 2.0 collective-permute-start.1
  24.1 16.8 %copy-start.27 = (s32[8]{0:T(128)S(1)}, s32[8]{0:T(128)}, u32[]{:S(2)}) copy-start(s32[8]{0:T(128)} %param.21) | copy-start | bytes 100
  24.1 16.8 %copy-start.25 = (bf16[128,512]{1,0:T(8,128)(2,1)S(1)}, bf16[128,512]{1,0:T(8,128)(2,1)}, u32[]{:S(2)}) copy-start(bf16[128,512]{1,0:T(8,128)(2,1)} %param.19) | copy-start | bytes 393220
  27.5 13.8 %copy-start.26 = (f32[4,128]{1,0:T(4,128)S(1)}, f32[4,128]{1,0:T(4,128)}, u32[]{:S(2)}) copy-start(f32[4,128]{1,0:T(4,128)} %param.23) | copy-start | bytes 6148
  37.4 18.6 %all-to-all-start = ((bf16[4,72,2048]{2,1,0:T(8,128)(2,1)}), bf16[4,72,2048]{2,1,0:T(8,128)(2,1)S(1)}, u32[]{:S(2)}, u32[]{:S(2)}) async-start(bf16[4,72,2048]{2,1,0:T(8,128)(2,1)} %select_scaled.4.refs_0_), calls=%async_computation | async-start | bytes 2359296 | tf_op jit(solution)/shard_map/all_to_all | solution.py:594
  67.2 4.9 %collective-permute-start.5 = (bf16[4,144,2048]{2,1,0:T(8,128)(2,1)}, bf16[4,144,2048]{2,1,0:T(8,128)(2,1)}, u32[]{:S(2)}, u32[]{:S(2)}) collective-permute-start(bf16[4,144,2048]{2,1,0:T(8,128)(2,1)} %bitcast.86), channel_id=1, source_target_pairs={{0,4},{4,0},{1,5},{5,1},{2,6},{6,2},{3,7},{7,3},{8,12},{12,8},{9,1... | collective-permute-start | bytes 7077896 | tf_op jit(solution)/shard_map/ppermute | solution.py:28
  67.3 12.6 %collective-permute-start.2 = (bf16[72,2048]{1,0:T(8,128)(2,1)}, bf16[72,2048]{1,0:T(8,128)(2,1)S(1)}, u32[]{:S(2)}, u32[]{:S(2)}) collective-permute-start(bf16[72,2048]{1,0:T(8,128)(2,1)} %get-tuple-element.78), channel_id=1, source_target_pairs={{0,1},{1,0},{2,3},{3,2},{4,5},{5,4},{6,7},{7,6},{8,9},{9,8},{10,11... | collective-permute-start | bytes 884744 | tf_op jit(solution)/shard_map/ppermute | solution.py:28
  68.8 15.6 %collective-permute-start.3 = (bf16[72,2048]{1,0:T(8,128)(2,1)}, bf16[72,2048]{1,0:T(8,128)(2,1)S(1)}, u32[]{:S(2)}, u32[]{:S(2)}) collective-permute-start(bf16[72,2048]{1,0:T(8,128)(2,1)} %get-tuple-element.79), channel_id=1, source_target_pairs={{0,2},{1,3},{2,0},{3,1},{4,6},{5,7},{6,4},{7,5},{8,10},{9,11},{10,... | collective-permute-start | bytes 884744 | tf_op jit(solution)/shard_map/ppermute | solution.py:28
  69.3 15.1 %collective-permute-start.4 = (bf16[72,2048]{1,0:T(8,128)(2,1)}, bf16[72,2048]{1,0:T(8,128)(2,1)S(1)}, u32[]{:S(2)}, u32[]{:S(2)}) collective-permute-start(bf16[72,2048]{1,0:T(8,128)(2,1)} %get-tuple-element.80), channel_id=1, source_target_pairs={{0,3},{1,2},{2,1},{3,0},{4,7},{5,6},{6,5},{7,4},{8,11},{9,10},{10,... | collective-permute-start | bytes 884744 | tf_op jit(solution)/shard_map/ppermute | solution.py:28
  85.2 45.0 %all-to-all-start.3 = ((bf16[4,3,72,2048]{3,2,1,0:T(8,128)(2,1)}), bf16[4,3,72,2048]{3,2,1,0:T(8,128)(2,1)}, u32[]{:S(2)}, u32[]{:S(2)}) async-start(bf16[4,3,72,2048]{3,2,1,0:T(8,128)(2,1)} %get-tuple-element.86), calls=%async_computation.3 | async-start | bytes 7077888 | tf_op jit(solution)/shard_map/all_to_all | solution.py:594
  109.2 4.4 %collective-permute-start.6 = (bf16[4,128,2048]{2,1,0:T(8,128)(2,1)}, bf16[4,128,2048]{2,1,0:T(8,128)(2,1)S(1)}, u32[]{:S(2)}, u32[]{:S(2)}) collective-permute-start(bf16[4,128,2048]{2,1,0:T(8,128)(2,1)} %bitcast.80), channel_id=1, source_target_pairs={{0,4},{4,0},{1,5},{5,1},{2,6},{6,2},{3,7},{7,3},{8,12},{12,8},{9,1... | collective-permute-start | bytes 6291464 | tf_op jit(solution)/shard_map/ppermute | solution.py:28
  130.2 18.0 %all-to-all-start.2 = ((bf16[4,72,2048]{2,1,0:T(8,128)(2,1)}), bf16[4,72,2048]{2,1,0:T(8,128)(2,1)S(1)}, u32[]{:S(2)}, u32[]{:S(2)}) async-start(bf16[4,72,2048]{2,1,0:T(8,128)(2,1)} %select_scaled.5.refs_0_), calls=%async_computation.2 | async-start | bytes 2359296 | tf_op jit(solution)/shard_map/all_to_all | solution.py:594
  149.3 18.0 %all-to-all-start.5 = ((bf16[4,72,2048]{2,1,0:T(8,128)(2,1)}), bf16[4,72,2048]{2,1,0:T(8,128)(2,1)S(1)}, u32[]{:S(2)}, u32[]{:S(2)}) async-start(bf16[4,72,2048]{2,1,0:T(8,128)(2,1)} %select_scaled.6.refs_4_), calls=%async_computation.5 | async-start | bytes 2359296 | tf_op jit(solution)/shard_map/all_to_all | solution.py:594
  168.3 29.8 %all-to-all-start.4 = ((bf16[4,72,2048]{2,1,0:T(8,128)(2,1)}), bf16[4,72,2048]{2,1,0:T(8,128)(2,1)S(1)}, u32[]{:S(2)}, u32[]{:S(2)}) async-start(bf16[4,72,2048]{2,1,0:T(8,128)(2,1)} %select_scaled.7.refs_4_), calls=%async_computation.4 | async-start | bytes 2359296 | tf_op jit(solution)/shard_map/all_to_all | solution.py:594
  171.8 130.6 %reduce-scatter.2.cloned.1.call-start = ((), (), s32[]{:S(2)}) async-start(), calls=%async_computation.7 | async-start | bytes 2621440 | tf_op jit(solution)/shard_map/reduce_scatter | solution.py:713
  185.0 10.3 %collective-permute-start.14 = (bf16[72,2048]{1,0:T(8,128)(2,1)}, bf16[72,2048]{1,0:T(8,128)(2,1)}, u32[]{:S(2)}, u32[]{:S(2)}) collective-permute-start(bf16[72,2048]{1,0:T(8,128)(2,1)} %get-tuple-element.115), channel_id=1, source_target_pairs={{0,1},{1,0},{2,3},{3,2},{4,5},{5,4},{6,7},{7,6},{8,9},{9,8},{10,11... | collective-permute-start | bytes 884744 | tf_op jit(solution)/shard_map/ppermute | solution.py:28
  187.0 25.8 %collective-permute-start.11 = (bf16[72,2048]{1,0:T(8,128)(2,1)}, bf16[72,2048]{1,0:T(8,128)(2,1)}, u32[]{:S(2)}, u32[]{:S(2)}) collective-permute-start(bf16[72,2048]{1,0:T(8,128)(2,1)} %get-tuple-element.112), channel_id=1, source_target_pairs={{0,1},{1,0},{2,3},{3,2},{4,5},{5,4},{6,7},{7,6},{8,9},{9,8},{10,11... | collective-permute-start | bytes 884744 | tf_op jit(solution)/shard_map/ppermute | solution.py:28
  187.1 22.0 %collective-permute-start.15 = (bf16[72,2048]{1,0:T(8,128)(2,1)}, bf16[72,2048]{1,0:T(8,128)(2,1)}, u32[]{:S(2)}, u32[]{:S(2)}) collective-permute-start(bf16[72,2048]{1,0:T(8,128)(2,1)} %get-tuple-element.116), channel_id=1, source_target_pairs={{0,2},{1,3},{2,0},{3,1},{4,6},{5,7},{6,4},{7,5},{8,10},{9,11},{10,... | collective-permute-start | bytes 884744 | tf_op jit(solution)/shard_map/ppermute | solution.py:28
  189.0 20.4 %collective-permute-start.16 = (bf16[72,2048]{1,0:T(8,128)(2,1)}, bf16[72,2048]{1,0:T(8,128)(2,1)}, u32[]{:S(2)}, u32[]{:S(2)}) collective-permute-start(bf16[72,2048]{1,0:T(8,128)(2,1)} %get-tuple-element.117), channel_id=1, source_target_pairs={{0,3},{1,2},{2,1},{3,0},{4,7},{5,6},{6,5},{7,4},{8,11},{9,10},{10,... | collective-permute-start | bytes 884744 | tf_op jit(solution)/shard_map/ppermute | solution.py:28
  190.5 23.2 %collective-permute-start.12 = (bf16[72,2048]{1,0:T(8,128)(2,1)}, bf16[72,2048]{1,0:T(8,128)(2,1)}, u32[]{:S(2)}, u32[]{:S(2)}) collective-permute-start(bf16[72,2048]{1,0:T(8,128)(2,1)} %get-tuple-element.113), channel_id=1, source_target_pairs={{0,2},{1,3},{2,0},{3,1},{4,6},{5,7},{6,4},{7,5},{8,10},{9,11},{10,... | collective-permute-start | bytes 884744 | tf_op jit(solution)/shard_map/ppermute | solution.py:28
  195.3 18.4 %collective-permute-start.13 = (bf16[72,2048]{1,0:T(8,128)(2,1)}, bf16[72,2048]{1,0:T(8,128)(2,1)}, u32[]{:S(2)}, u32[]{:S(2)}) collective-permute-start(bf16[72,2048]{1,0:T(8,128)(2,1)} %get-tuple-element.114), channel_id=1, source_target_pairs={{0,3},{1,2},{2,1},{3,0},{4,7},{5,6},{6,5},{7,4},{8,11},{9,10},{10,... | collective-permute-start | bytes 884744 | tf_op jit(solution)/shard_map/ppermute | solution.py:28
  218.5 1.6 collective-permute-start.17
  220.2 13.3 %collective-permute-start.18 = (bf16[128,1024]{1,0:T(8,128)(2,1)S(1)}, bf16[128,1024]{1,0:T(8,128)(2,1)S(1)}, u32[]{:S(2)}, u32[]{:S(2)}) collective-permute-start(bf16[128,1024]{1,0:T(8,128)(2,1)S(1)} %add_convert_fusion.7), channel_id=1, source_target_pairs={{0,8},{8,0},{16,24},{24,16},{1,9},{9,1},{17,25},{25,17},{2,10},{10... | collective-permute-start | bytes 786440 | tf_op jit(solution)/shard_map/ppermute | solution.py:28
  221.7 14.0 %collective-permute-start.10 = (bf16[72,2048]{1,0:T(8,128)(2,1)}, bf16[72,2048]{1,0:T(8,128)(2,1)S(1)}, u32[]{:S(2)}, u32[]{:S(2)}) collective-permute-start(bf16[72,2048]{1,0:T(8,128)(2,1)} %get-tuple-element.109), channel_id=1, source_target_pairs={{0,3},{1,2},{2,1},{3,0},{4,7},{5,6},{6,5},{7,4},{8,11},{9,10},{10,... | collective-permute-start | bytes 884744 | tf_op jit(solution)/shard_map/ppermute | solution.py:28
  224.3 14.0 %collective-permute-start.8 = (bf16[72,2048]{1,0:T(8,128)(2,1)}, bf16[72,2048]{1,0:T(8,128)(2,1)}, u32[]{:S(2)}, u32[]{:S(2)}) collective-permute-start(bf16[72,2048]{1,0:T(8,128)(2,1)} %get-tuple-element.107), channel_id=1, source_target_pairs={{0,1},{1,0},{2,3},{3,2},{4,5},{5,4},{6,7},{7,6},{8,9},{9,8},{10,11... | collective-permute-start | bytes 884744 | tf_op jit(solution)/shard_map/ppermute | solution.py:28
  224.8 13.4 %collective-permute-start.9 = (bf16[72,2048]{1,0:T(8,128)(2,1)}, bf16[72,2048]{1,0:T(8,128)(2,1)}, u32[]{:S(2)}, u32[]{:S(2)}) collective-permute-start(bf16[72,2048]{1,0:T(8,128)(2,1)} %get-tuple-element.108), channel_id=1, source_target_pairs={{0,2},{1,3},{2,0},{3,1},{4,6},{5,7},{6,4},{7,5},{8,10},{9,11},{10,... | collective-permute-start | bytes 884744 | tf_op jit(solution)/shard_map/ppermute | solution.py:28
  225.2 18.9 %collective-permute-start.7 = (bf16[128,2048]{1,0:T(8,128)(2,1)S(1)}, bf16[128,2048]{1,0:T(8,128)(2,1)}, u32[]{:S(2)}, u32[]{:S(2)}) collective-permute-start(bf16[128,2048]{1,0:T(8,128)(2,1)S(1)} %copy-done.14), channel_id=1, source_target_pairs={{0,4},{4,0},{1,5},{5,1},{2,6},{6,2},{3,7},{7,3},{8,12},{12,8},{9,1... | collective-permute-start | bytes 1572872 | tf_op jit(solution)/shard_map/ppermute | solution.py:28
  225.2 9.0 %copy-start.15 = (bf16[128,2048]{1,0:T(8,128)(2,1)S(1)}, bf16[128,2048]{1,0:T(8,128)(2,1)}, u32[]{:S(2)}) copy-start(bf16[128,2048]{1,0:T(8,128)(2,1)} %get-tuple-element.121) | copy-start | bytes 1572868
  233.5 10.6 %copy-start.2 = (f32[128,2048]{1,0:T(8,128)S(1)}, f32[128,2048]{1,0:T(8,128)}, u32[]{:S(2)}) copy-start(f32[128,2048]{1,0:T(8,128)} %get-tuple-element.119.refs_0_) | copy-start | bytes 3145732
  233.5 10.6 %copy-start.11 = (f32[128,2048]{1,0:T(8,128)S(1)}, f32[128,2048]{1,0:T(8,128)}, u32[]{:S(2)}) copy-start(f32[128,2048]{1,0:T(8,128)} %get-tuple-element.118.refs_4_) | copy-start | bytes 3145732
  234.2 9.9 %collective-permute-start.21 = (bf16[128,2048]{1,0:T(8,128)(2,1)S(1)}, bf16[128,2048]{1,0:T(8,128)(2,1)S(1)}, u32[]{:S(2)}, u32[]{:S(2)}) collective-permute-start(bf16[128,2048]{1,0:T(8,128)(2,1)S(1)} %copy-done.15), channel_id=1, source_target_pairs={{0,4},{4,0},{1,5},{5,1},{2,6},{6,2},{3,7},{7,3},{8,12},{12,8},{9,1... | collective-permute-start | bytes 1572872 | tf_op jit(solution)/shard_map/ppermute | solution.py:28
  235.7 8.4 %collective-permute-start.20 = (bf16[128,2048]{1,0:T(8,128)(2,1)}, bf16[128,2048]{1,0:T(8,128)(2,1)}, u32[]{:S(2)}, u32[]{:S(2)}) collective-permute-start(bf16[128,2048]{1,0:T(8,128)(2,1)} %get-tuple-element.125), channel_id=1, source_target_pairs={{0,4},{4,0},{1,5},{5,1},{2,6},{6,2},{3,7},{7,3},{8,12},{12,8},{9,1... | collective-permute-start | bytes 1572872 | tf_op jit(solution)/shard_map/ppermute | solution.py:28
  241.4 2.7 collective-permute-start.19
  241.4 15.3 %collective-permute-start.22 = (bf16[128,1024]{1,0:T(8,128)(2,1)S(1)}, bf16[128,1024]{1,0:T(8,128)(2,1)}, u32[]{:S(2)}, u32[]{:S(2)}) collective-permute-start(bf16[128,1024]{1,0:T(8,128)(2,1)S(1)} %add_convert_fusion.6), channel_id=1, source_target_pairs={{0,16},{8,24},{16,0},{24,8},{1,17},{9,25},{17,1},{25,9},{2,18},{10... | collective-permute-start | bytes 786440 | tf_op jit(solution)/shard_map/ppermute | solution.py:28
  257.8 8.9 %collective-permute-start.23 = (bf16[128,1024]{1,0:T(8,128)(2,1)S(1)}, bf16[128,1024]{1,0:T(8,128)(2,1)S(1)}, u32[]{:S(2)}, u32[]{:S(2)}) collective-permute-start(bf16[128,1024]{1,0:T(8,128)(2,1)S(1)} %fusion.7), channel_id=1, source_target_pairs={{3,2},{7,6},{11,10},{15,14},{19,18},{23,22},{27,26},{31,30}} | collective-permute-start | bytes 786440 | tf_op jit(solution)/shard_map/ppermute | solution.py:726
  258.5 18.6 %copy-start.16 = (bf16[128,512]{1,0:T(8,128)(2,1)S(1)}, bf16[128,512]{1,0:T(8,128)(2,1)}, u32[]{:S(2)}) copy-start(bf16[128,512]{1,0:T(8,128)(2,1)} %param.22) | copy-start | bytes 393220
  266.9 10.1 %collective-permute-start.24 = (bf16[128,1024]{1,0:T(8,128)(2,1)S(1)}, bf16[128,1024]{1,0:T(8,128)(2,1)S(1)}, u32[]{:S(2)}, u32[]{:S(2)}) collective-permute-start(bf16[128,1024]{1,0:T(8,128)(2,1)S(1)} %add.134), channel_id=1, source_target_pairs={{3,1},{2,0},{7,5},{6,4},{11,9},{10,8},{15,13},{14,12},{19,17},{18,... | collective-permute-start | bytes 786440 | tf_op jit(solution)/shard_map/ppermute | solution.py:726
  277.0 8.6 %collective-permute-start.25 = (bf16[128,1024]{1,0:T(8,128)(2,1)S(1)}, bf16[128,1024]{1,0:T(8,128)(2,1)}, u32[]{:S(2)}, u32[]{:S(2)}) collective-permute-start(bf16[128,1024]{1,0:T(8,128)(2,1)S(1)} %add.135), channel_id=1, source_target_pairs={{0,4},{4,0},{1,5},{5,1},{2,6},{6,2},{3,7},{7,3},{8,12},{12,8},{9,1... | collective-permute-start | bytes 786440 | tf_op jit(solution)/shard_map/ppermute | solution.py:28
  290.0 5.2 %collective-permute-start.26 = (bf16[1024,128]{1,0:T(8,128)(2,1)S(1)}, bf16[1024,128]{1,0:T(8,128)(2,1)S(1)}, u32[]{:S(2)}, u32[]{:S(2)}) collective-permute-start(bf16[1024,128]{1,0:T(8,128)(2,1)S(1)} %get-tuple-element.168), channel_id=1, source_target_pairs={{0,4},{4,0},{1,5},{5,1},{2,6},{6,2},{3,7},{7,3},{8,12},{12,8},{9,1... | collective-permute-start | bytes 786440 | tf_op jit(solution)/shard_map/ppermute | solution.py:28
  291.7 9.2 %collective-permute-start.27 = (f32[32,512]{1,0:T(8,128)}, f32[32,512]{1,0:T(8,128)}, u32[]{:S(2)}, u32[]{:S(2)}) collective-permute-start(f32[32,512]{1,0:T(8,128)} %get-tuple-element.165), channel_id=1, source_target_pairs={{0,1},{1,0},{2,3},{3,2},{4,5},{5,4},{6,7},{7,6},{8,9},{9,8},{10,11... | collective-permute-start | bytes 196616 | tf_op jit(solution)/shard_map/ppermute | solution.py:28
  293.7 7.2 %collective-permute-start.28 = (f32[32,512]{1,0:T(8,128)}, f32[32,512]{1,0:T(8,128)}, u32[]{:S(2)}, u32[]{:S(2)}) collective-permute-start(f32[32,512]{1,0:T(8,128)} %get-tuple-element.167), channel_id=1, source_target_pairs={{0,2},{1,3},{2,0},{3,1},{4,6},{5,7},{6,4},{7,5},{8,10},{9,11},{10,... | collective-permute-start | bytes 196616 | tf_op jit(solution)/shard_map/ppermute | solution.py:28
  293.7 7.2 %collective-permute-start.29 = (f32[32,512]{1,0:T(8,128)}, f32[32,512]{1,0:T(8,128)}, u32[]{:S(2)}, u32[]{:S(2)}) collective-permute-start(f32[32,512]{1,0:T(8,128)} %get-tuple-element.166), channel_id=1, source_target_pairs={{0,3},{1,2},{2,1},{3,0},{4,7},{5,6},{6,5},{7,4},{8,11},{9,10},{10,... | collective-permute-start | bytes 196616 | tf_op jit(solution)/shard_map/ppermute | solution.py:28
  295.9 6.5 %collective-permute-start.30 = (bf16[1024,128]{1,0:T(8,128)(2,1)}, bf16[1024,128]{1,0:T(8,128)(2,1)}, u32[]{:S(2)}, u32[]{:S(2)}) collective-permute-start(bf16[1024,128]{1,0:T(8,128)(2,1)} %add_convert_fusion.4), channel_id=1, source_target_pairs={{0,0},{4,16},{8,4},{12,20},{16,8},{20,24},{24,12},{28,28},{1,1},{5... | collective-permute-start | bytes 786440 | tf_op jit(solution)/shard_map/ppermute | solution.py:805
  (20 other events, 60.3 us)
Sparse Core Ops, SparseCore 0:
  9.6 53.1 all-gather.6
  64.4 44.7 all-gather.4
  256.9 43.7 reduce-scatter.1

commit v2 on v1

--- a/solution.py
+++ b/solution.py
@@ -697,15 +697,17 @@
     run_total(0)
     run_total(1)
     run_total(2)
+    run_combine(3)
+    run_total(3)
     scaled, hidden, d_gate, d_up = kept
+    arrived = swap(held, "z", 1)
     grad_down, state["after"] = weight_grad(hidden, scaled, 384, state["after"])
-    held = (held.astype(F32) + swap(held, "z", 1).astype(F32)).astype(BF)
+    held = (held.astype(F32) + after(arrived, state["after"]).astype(F32)).astype(BF)
     then(held)
-    run_combine(3)
     arrived = swap(held, "z", 2)
-    held = (held.astype(F32) + arrived.astype(F32)).astype(BF)
+    grads, state["after"] = weight_grad(ins, d_gate, 512, state["after"], 0, 2)
+    held = (held.astype(F32) + after(arrived, state["after"]).astype(F32)).astype(BF)
     held = jnp.where(key == n_key - 1, held, jnp.zeros_like(held))
-    run_total(3)
     by_height = [
         pick(z, [totals[0 if at == to else ORDER[at].index(to) + 1] for at in range(n_z)])
         for to in range(n_z)
@@ -717,8 +719,7 @@
         tiled=True,
     )
     then(held)
-    work = [(d_gate, 0), (d_up, 1)]
-    grads = None
+    work = [(d_up, 1)]
     sources = [n_key - 1]
     bit = 1
     while bit < n_key:
@@ -728,7 +729,6 @@
             right, part = work.pop(0)
             grads, state["after"] = weight_grad(ins, right, 512, state["after"], part, 2, grads)
         held = held + after(arrived, state["after"])
-        then(held)
         sources += [target for _, target in route]
         bit *= 2
     for right, part in work:

time: 316 us -> 314 us (level)
  transfers between devices with their start and end apart: 40 -> 40, of which waited for: 18 -> 17; matrix products, arithmetic and copies ran while one was open for 6% -> 6% of each run, Pallas kernels for 37% -> 38%
where the time goes in v2:
time: 314 us; the launch traced here: 312 us
  Pallas kernels  121 us (39%)
  waiting for transfers between devices  88.8 us (28%)
  starting transfers between devices  57.2 us (18%)
  between operations  14.3 us (5%)
  local copies, waits for them, and re-layouts  13.2 us (4%)
  other arithmetic  12.7 us (4%)
  matrix products  4.87 us (2%)
    pallas_call x4, Pallas kernels, expert(): pl.pallas_call(functools.partial(expert_kernel, n_key), grid=(steps,), ou...  40 us
    all_to_all x6, waiting for transfers between devices, exchange(): return lax.all_to_all(x, 'key', split_axis=0, concat_axis=0, tiled=True)  30.3 us
    ppermute x28, waiting for transfers between devices, swap(): return lax.ppermute(block, axis, [(i, i ^ mask) for i in range(count)])  28.8 us
    ppermute x28, starting transfers between devices, swap(): return lax.ppermute(block, axis, [(i, i ^ mask) for i in range(count)])  27.4 us
    pallas_call x3, Pallas kernels, weight_grad(): pl.pallas_call(weights_kernel, grid=(height // tile,), out_shape=[jax.Sha...  24.6 us
    all_to_all x6, starting transfers between devices, exchange(): return lax.all_to_all(x, 'key', split_axis=0, concat_axis=0, tiled=True)  24.1 us
    all_gather x1, waiting for transfers between devices, layer(): column_up = lax.all_gather(upstream, 'z')  19.2 us
    pallas_call x2, Pallas kernels, gate_up(): pl.pallas_call(functools.partial(gate_kernel, n_key, count), grid=(steps,...  16.4 us
  transfers between devices with their start and end apart: 40, of which 17 were waited for; matrix products, arithmetic and copies ran while one was open for 6% of the time, Pallas kernels for 38%

profile of v2, /device:TPU:0, one launch (start us, length us, event | category | flops | bytes accessed | tf_op | source)
XLA Modules:
  0.0 312.0 jit_solution(10052359236975327292)
XLA Ops:
  7.2 2.1 build_block.1.after
  12.5 3.7 %select_inputs.2 = (bf16[4,1,72,2048]{3,2,1,0:T(8,128)(2,1)}, bf16[1,288,256]{2,1,0:T(8,128)(2,1)}, f32[1,288,128]{2,1,0:T(8,128)}) custom-call(s32[2]{0:T(128)} %pad_add_fusion.meta, bf16[1,144,2048]{2,1,0:T(8,128)(2,1)} %bitcast.84, bf16[1,144,2048]{2,1,0:T(8,128)(2,1)} %bitcast.91, bf16[1,144,2048]{2,1,0:T(8,128)(2,1)} %bitcast.85, ...), custom_call_target="tpu_custom_call" | custom-call | flops 1000 | bytes 1000 | tf_op jit(solution)/shard_map/select_inputs/pallas_call | solution.py:304
  16.2 5.1 %all-to-all-start.1 = ((bf16[4,1,72,2048]{3,2,1,0:T(8,128)(2,1)}), bf16[4,1,72,2048]{3,2,1,0:T(8,128)(2,1)}, u32[]{:S(2)}, u32[]{:S(2)}) async-start(bf16[4,1,72,2048]{3,2,1,0:T(8,128)(2,1)} %get-tuple-element.78), calls=%async_computation.1 | async-start | bytes 2359296 | tf_op jit(solution)/shard_map/all_to_all | solution.py:594
  24.1 3.4 %select_scaled.4.refs_0_ = bf16[4,72,2048]{2,1,0:T(8,128)(2,1)} custom-call(s32[2]{0:T(128)} %pad_add_fusion.meta, bf16[1,128,2048]{2,1,0:T(8,128)(2,1)} %bitcast.89, bf16[1,128,2048]{2,1,0:T(8,128)(2,1)} %bitcast.100, bf16[1,288,256]{2,1,0:T(8,128)(2,1)} %get-tuple-element.76.hot_ref.after, f32[1,288,128]{2,1,0:T(8,128)} %get-tuple-element.77.scale_ref, ...), custom_call_target="tpu_custom_call" | custom-call | flops 1000 | bytes 1000 | tf_op jit(solution)/shard_map/select_scaled/pallas_call | solution.py:351
  27.5 9.8 %all-to-all-done.1.pieces = bf16[4,1,72,2048]{3,2,1,0:T(8,128)(2,1)} async-done(((bf16[4,1,72,2048]{3,2,1,0:T(8,128)(2,1)}), bf16[4,1,72,2048]{3,2,1,0:T(8,128)(2,1)}, u32[]{:S(2)}, u32[]{:S(2)}) %all-to-all-start.1) | async-done | bytes 1179680 | tf_op jit(solution)/shard_map/all_to_all | solution.py:594
  37.4 3.5 %all-to-all-start = ((bf16[4,72,2048]{2,1,0:T(8,128)(2,1)}), bf16[4,72,2048]{2,1,0:T(8,128)(2,1)S(1)}, u32[]{:S(2)}, u32[]{:S(2)}) async-start(bf16[4,72,2048]{2,1,0:T(8,128)(2,1)} %select_scaled.4.refs_0_), calls=%async_computation | async-start | bytes 2359296 | tf_op jit(solution)/shard_map/all_to_all | solution.py:594
  41.3 1.9 bitcast_select_fusion
  43.2 5.9 %gate_up.2 = (bf16[1152,2048]{1,0:T(8,128)(2,1)}, f32[288,768]{1,0:T(8,128)}, f32[288,768]{1,0:T(8,128)}) custom-call(bf16[4,1,72,2048]{3,2,1,0:T(8,128)(2,1)} %all-to-all-done.1.pieces, bf16[2048,1536]{1,0:T(8,128)(2,1)} %bitcast.64, bf16[2048,1536]{1,0:T(8,128)(2,1)} %bitcast.65, bf16[4,72,2048]{2,1,0:T(8,128)(2,1)} %select_scaled.4.refs_0_), custom_call_target="tpu_custom_call" | custom-call | flops 1000 | bytes 1000 | tf_op jit(solution)/shard_map/gate_up/pallas_call | solution.py:391
  49.2 6.8 %all-to-all-done.pieces = bf16[4,72,2048]{2,1,0:T(8,128)(2,1)S(1)} async-done(((bf16[4,72,2048]{2,1,0:T(8,128)(2,1)}), bf16[4,72,2048]{2,1,0:T(8,128)(2,1)S(1)}, u32[]{:S(2)}, u32[]{:S(2)}) %all-to-all-start) | async-done | bytes 1179680 | tf_op jit(solution)/shard_map/all_to_all | solution.py:594
  57.0 10.2 %expert_chunk.4 = (bf16[72,2048]{1,0:T(8,128)(2,1)}, bf16[72,2048]{1,0:T(8,128)(2,1)}, bf16[72,2048]{1,0:T(8,128)(2,1)}, bf16[72,2048]{1,0:T(8,128)(2,1)}, bf16[...) custom-call(s32[1]{0:T(128)} %bitcast.meta, ...), custom_call_target="tpu_custom_call" | custom-call | flops 1000 | bytes 1000 | tf_op jit(solution)/shard_map/expert_chunk/pallas_call | solution.py:461
  72.1 7.7 %select_inputs.3 = (bf16[4,3,72,2048]{3,2,1,0:T(8,128)(2,1)}, bf16[3,288,256]{2,1,0:T(8,128)(2,1)}, f32[3,288,128]{2,1,0:T(8,128)}) custom-call(s32[4]{0:T(128)} %pad_add_fusion.1.meta, bf16[4,144,2048]{2,1,0:T(8,128)(2,1)} %bitcast.87, bf16[4,144,2048]{2,1,0:T(8,128)(2,1)} %collective-permute-done.5.xb.ib, bf16[4,144,2048]{2,1,0:T(8,128)(2,1)} %bitcast.88, ...), custom_call_target="tpu_custom_call" | custom-call | flops 1000 | bytes 1000 | tf_op jit(solution)/shard_map/select_inputs/pallas_call | solution.py:304
  79.8 4.5 %collective-permute-done.3.refs_2_ = bf16[72,2048]{1,0:T(8,128)(2,1)S(1)} collective-permute-done((bf16[72,2048]{1,0:T(8,128)(2,1)}, bf16[72,2048]{1,0:T(8,128)(2,1)S(1)}, u32[]{:S(2)}, u32[]{:S(2)}) %collective-permute-start.3) | collective-permute-done | bytes 294944 | tf_op jit(solution)/shard_map/ppermute | solution.py:28
  85.2 4.7 %all-to-all-start.3 = ((bf16[4,3,72,2048]{3,2,1,0:T(8,128)(2,1)}), bf16[4,3,72,2048]{3,2,1,0:T(8,128)(2,1)}, u32[]{:S(2)}, u32[]{:S(2)}) async-start(bf16[4,3,72,2048]{3,2,1,0:T(8,128)(2,1)} %get-tuple-element.90), calls=%async_computation.3 | async-start | bytes 7077888 | tf_op jit(solution)/shard_map/all_to_all | solution.py:594
  89.9 19.2 %all-gather.5.cloned.1.call-done = bf16[512,2048]{1,0:T(8,128)(2,1)} async-done(((bf16[128,2048]{1,0:T(8,128)(2,1)}), bf16[512,2048]{1,0:T(8,128)(2,1)}) %all-gather.5.cloned.1.call-update) | async-done | bytes 2097168 | tf_op jit(solution)/shard_map/all_gather | solution.py:586
  109.2 4.4 %collective-permute-done.6.xb = bf16[4,128,2048]{2,1,0:T(8,128)(2,1)S(1)} collective-permute-done((bf16[4,128,2048]{2,1,0:T(8,128)(2,1)}, bf16[4,128,2048]{2,1,0:T(8,128)(2,1)S(1)}, u32[]{:S(2)}, u32[]{:S(2)}) %collective-permute-start.6) | collective-permute-done | bytes 2097184 | tf_op jit(solution)/shard_map/ppermute | solution.py:28
  114.8 3.3 %select_scaled.5.refs_0_ = bf16[4,72,2048]{2,1,0:T(8,128)(2,1)} custom-call(s32[4]{0:T(128)} %pad_add_fusion.1.meta, bf16[4,128,2048]{2,1,0:T(8,128)(2,1)} %bitcast.81, bf16[4,128,2048]{2,1,0:T(8,128)(2,1)} %copy-done.1, bf16[3,288,256]{2,1,0:T(8,128)(2,1)} %get-tuple-element.86.hot_ref.after, f32[3,288,128]{2,1,0:T(8,128)} %get-tuple-element.88.scale_ref, ...), custom_call_target="tpu_custom_call" | custom-call | flops 1000 | bytes 1000 | tf_op jit(solution)/shard_map/select_scaled/pallas_call | solution.py:351
  118.2 12.0 %all-to-all-done.3.pieces = bf16[4,3,72,2048]{3,2,1,0:T(8,128)(2,1)} async-done(((bf16[4,3,72,2048]{3,2,1,0:T(8,128)(2,1)}), bf16[4,3,72,2048]{3,2,1,0:T(8,128)(2,1)}, u32[]{:S(2)}, u32[]{:S(2)}) %all-to-all-start.3) | async-done | bytes 3538976 | tf_op jit(solution)/shard_map/all_to_all | solution.py:594
  130.2 3.5 %all-to-all-start.2 = ((bf16[4,72,2048]{2,1,0:T(8,128)(2,1)}), bf16[4,72,2048]{2,1,0:T(8,128)(2,1)S(1)}, u32[]{:S(2)}, u32[]{:S(2)}) async-start(bf16[4,72,2048]{2,1,0:T(8,128)(2,1)} %select_scaled.5.refs_0_), calls=%async_computation.2 | async-start | bytes 2359296 | tf_op jit(solution)/shard_map/all_to_all | solution.py:594
  133.8 10.5 %gate_up.3 = (bf16[1152,2048]{1,0:T(8,128)(2,1)}, f32[864,768]{1,0:T(8,128)}, f32[864,768]{1,0:T(8,128)}) custom-call(bf16[4,3,72,2048]{3,2,1,0:T(8,128)(2,1)} %all-to-all-done.3.pieces, bf16[2048,1536]{1,0:T(8,128)(2,1)} %bitcast.68, bf16[2048,1536]{1,0:T(8,128)(2,1)} %bitcast.69, ...), custom_call_target="tpu_custom_call", output_to_operand_aliasing={{0}: (4, {})} | custom-call | flops 1000 | bytes 1000 | tf_op jit(solution)/shard_map/gate_up/pallas_call | solution.py:391
  144.2 3.3 %select_scaled.6.refs_4_ = bf16[4,72,2048]{2,1,0:T(8,128)(2,1)} custom-call(s32[4]{0:T(128)} %pad_add_fusion.1.meta, bf16[4,128,2048]{2,1,0:T(8,128)(2,1)} %bitcast.82, bf16[4,128,2048]{2,1,0:T(8,128)(2,1)} %copy-done.1, bf16[3,288,256]{2,1,0:T(8,128)(2,1)} %get-tuple-element.86.hot_ref.after, f32[3,288,128]{2,1,0:T(8,128)} %get-tuple-element.88.scale_ref, ...), custom_call_target="tpu_custom_call" | custom-call | flops 1000 | bytes 1000 | tf_op jit(solution)/shard_map/select_scaled/pallas_call | solution.py:351
  149.3 3.7 %all-to-all-start.5 = ((bf16[4,72,2048]{2,1,0:T(8,128)(2,1)}), bf16[4,72,2048]{2,1,0:T(8,128)(2,1)S(1)}, u32[]{:S(2)}, u32[]{:S(2)}) async-start(bf16[4,72,2048]{2,1,0:T(8,128)(2,1)} %select_scaled.6.refs_4_), calls=%async_computation.5 | async-start | bytes 2359296 | tf_op jit(solution)/shard_map/all_to_all | solution.py:594
  153.0 10.0 %expert_chunk.5 = (bf16[72,2048]{1,0:T(8,128)(2,1)}, bf16[72,2048]{1,0:T(8,128)(2,1)}, bf16[72,2048]{1,0:T(8,128)(2,1)}, bf16[72,2048]{1,0:T(8,128)(2,1)}, bf16[...) custom-call(s32[1]{0:T(128)} %bitcast.meta, ...), custom_call_target="tpu_custom_call", output_to_operand_aliasing={{4}: (7, {}), {5}: (8, {}), {6}: (9, {}), {7}: (10, {})} | custom-call | flops 1000 | bytes 1000 | tf_op jit(solution)/shard_map/expert_chunk/pallas_call | solution.py:461
  163.0 3.3 %select_scaled.7.refs_4_ = bf16[4,72,2048]{2,1,0:T(8,128)(2,1)} custom-call(s32[4]{0:T(128)} %pad_add_fusion.1.meta, bf16[4,128,2048]{2,1,0:T(8,128)(2,1)} %bitcast.83, bf16[4,128,2048]{2,1,0:T(8,128)(2,1)} %copy-done.1, bf16[3,288,256]{2,1,0:T(8,128)(2,1)} %get-tuple-element.86.hot_ref.after, f32[3,288,128]{2,1,0:T(8,128)} %get-tuple-element.88.scale_ref, ...), custom_call_target="tpu_custom_call" | custom-call | flops 1000 | bytes 1000 | tf_op jit(solution)/shard_map/select_scaled/pallas_call | solution.py:351
  168.3 3.5 %all-to-all-start.4 = ((bf16[4,72,2048]{2,1,0:T(8,128)(2,1)}), bf16[4,72,2048]{2,1,0:T(8,128)(2,1)S(1)}, u32[]{:S(2)}, u32[]{:S(2)}) async-start(bf16[4,72,2048]{2,1,0:T(8,128)(2,1)} %select_scaled.7.refs_4_), calls=%async_computation.4 | async-start | bytes 2359296 | tf_op jit(solution)/shard_map/all_to_all | solution.py:594
  171.9 3.2 %combine_rows.4 = (f32[128,2048]{1,0:T(8,128)}, bf16[128,2048]{1,0:T(8,128)(2,1)}) custom-call(s32[1]{0:T(128)} %bitcast.meta, bf16[1,288,256]{2,1,0:T(8,128)(2,1)} %get-tuple-element.76.hot_ref.after, bf16[72,2048]{1,0:T(8,128)(2,1)} %get-tuple-element.81.after.refs_0_, bf16[72,2048]{1,0:T(8,128)(2,1)} %copy-done.22, bf16[72,2048]{1,0:T(8,128)(2,1)} %copy-done.23, ...), custom_call_target="tpu_custom_call" | custom-call | flops 1000 | bytes 1000 | tf_op jit(solution)/shard_map/combine_rows/pallas_call | solution.py:547
  175.1 9.9 %expert_chunk.6 = (bf16[72,2048]{1,0:T(8,128)(2,1)}, bf16[72,2048]{1,0:T(8,128)(2,1)}, bf16[72,2048]{1,0:T(8,128)(2,1)}, bf16[72,2048]{1,0:T(8,128)(2,1)}, bf16[...) custom-call(s32[1]{0:T(128)} %bitcast.meta, ...), custom_call_target="tpu_custom_call", output_to_operand_aliasing={{4}: (7, {}), {5}: (8, {}), {6}: (9, {}), {7}: (10, {})} | custom-call | flops 1000 | bytes 1000 | tf_op jit(solution)/shard_map/expert_chunk/pallas_call | solution.py:461
  185.0 1.9 collective-permute-start.14
  188.5 1.9 collective-permute-start.11
  191.9 3.4 %collective-permute-done.14.refs_1_ = bf16[72,2048]{1,0:T(8,128)(2,1)} collective-permute-done((bf16[72,2048]{1,0:T(8,128)(2,1)}, bf16[72,2048]{1,0:T(8,128)(2,1)}, u32[]{:S(2)}, u32[]{:S(2)}) %collective-permute-start.14) | collective-permute-done | bytes 294944 | tf_op jit(solution)/shard_map/ppermute | solution.py:28
  195.3 2.8 collective-permute-start.13
  199.2 9.9 %expert_chunk.7 = (bf16[72,2048]{1,0:T(8,128)(2,1)}, bf16[72,2048]{1,0:T(8,128)(2,1)}, bf16[72,2048]{1,0:T(8,128)(2,1)}, bf16[72,2048]{1,0:T(8,128)(2,1)}, bf16[...) custom-call(s32[1]{0:T(128)} %bitcast.meta, ...), custom_call_target="tpu_custom_call", output_to_operand_aliasing={{4}: (7, {}), {5}: (8, {}), {6}: (9, {}), {7}: (10, {})} | custom-call | flops 1000 | bytes 1000 | tf_op jit(solution)/shard_map/expert_chunk/pallas_call | solution.py:461
  209.3 1.9 collective-permute-start.8
  211.2 3.3 %combine_rows.5 = (f32[128,2048]{1,0:T(8,128)}, bf16[128,2048]{1,0:T(8,128)(2,1)}) custom-call(s32[1]{0:T(128)} %bitcast.meta, bf16[3,288,256]{2,1,0:T(8,128)(2,1)} %get-tuple-element.86.hot_ref.after, bf16[72,2048]{1,0:T(8,128)(2,1)} %get-tuple-element.109.refs_4_.refs_0_, bf16[72,2048]{1,0:T(8,128)(2,1)} %collective-permute-done.14.refs_1_, ...), custom_call_target="tpu_custom_call" | custom-call | flops 1000 | bytes 1000 | tf_op jit(solution)/shard_map/combine_rows/pallas_call | solution.py:547
  216.0 3.9 %collective-permute-done.12.refs_2_ = bf16[72,2048]{1,0:T(8,128)(2,1)} collective-permute-done((bf16[72,2048]{1,0:T(8,128)(2,1)}, bf16[72,2048]{1,0:T(8,128)(2,1)}, u32[]{:S(2)}, u32[]{:S(2)}) %collective-permute-start.12) | collective-permute-done | bytes 294944 | tf_op jit(solution)/shard_map/ppermute | solution.py:28
  219.9 3.3 %combine_rows.6 = (f32[128,2048]{1,0:T(8,128)}, bf16[128,2048]{1,0:T(8,128)(2,1)}) custom-call(s32[1]{0:T(128)} %bitcast.meta, bf16[3,288,256]{2,1,0:T(8,128)(2,1)} %get-tuple-element.86.hot_ref.after, bf16[72,2048]{1,0:T(8,128)(2,1)} %get-tuple-element.98.after.refs_0_, bf16[72,2048]{1,0:T(8,128)(2,1)} %collective-permute-done.11.refs_1_, ...), custom_call_target="tpu_custom_call" | custom-call | flops 1000 | bytes 1000 | tf_op jit(solution)/shard_map/combine_rows/pallas_call | solution.py:547
  226.9 3.3 %combine_rows.7 = (f32[128,2048]{1,0:T(8,128)}, bf16[128,2048]{1,0:T(8,128)(2,1)}) custom-call(s32[1]{0:T(128)} %bitcast.meta, bf16[3,288,256]{2,1,0:T(8,128)(2,1)} %get-tuple-element.86.hot_ref.after, bf16[72,2048]{1,0:T(8,128)(2,1)} %get-tuple-element.110.refs_4_.refs_0_, bf16[72,2048]{1,0:T(8,128)(2,1)} %copy-done.20, bf16[72,2048]{1,0:T(8,128)(2,1)} %copy-done.21, ...), custom_call_target="tpu_custom_call" | custom-call | flops 1000 | bytes 1000 | tf_op jit(solution)/shard_map/combine_rows/pallas_call | solution.py:547
  232.3 8.4 %weight_gradient.3 = (bf16[768,2048]{1,0:T(8,128)(2,1)}, f32[8,128]{1,0:T(8,128)}) custom-call(bf16[1152,768]{1,0:T(8,128)(2,1)} %get-tuple-element.126.left_ref, bf16[1152,2048]{1,0:T(8,128)(2,1)} %get-tuple-element.127.right_ref, f32[128,2048]{1,0:T(8,128)} %get-tuple-element.122.refs_0_), custom_call_target="tpu_custom_call" | custom-call | flops 1000 | bytes 1000 | tf_op jit(solution)/shard_map/weight_gradient/pallas_call | solution.py:501
  240.7 2.7 collective-permute-start.22
  243.4 2.1 select_select_fusion.3
  245.8 1.6 pad_maximum_fusion
  247.4 7.9 %collective-permute-done.22 = bf16[128,1024]{1,0:T(8,128)(2,1)S(1)} collective-permute-done((bf16[128,1024]{1,0:T(8,128)(2,1)S(1)}, bf16[128,1024]{1,0:T(8,128)(2,1)S(1)}, u32[]{:S(2)}, u32[]{:S(2)}) %collective-permute-start.22) | collective-permute-done | bytes 262176 | tf_op jit(solution)/shard_map/ppermute | solution.py:28
  255.3 8.1 %weight_gradient.4 = (bf16[2048,1536]{1,0:T(8,128)(2,1)}, f32[8,128]{1,0:T(8,128)}) custom-call(bf16[1152,2048]{1,0:T(8,128)(2,1)} %get-tuple-element.131.left_ref, bf16[1152,768]{1,0:T(8,128)(2,1)} %get-tuple-element.132.right_ref, f32[8,128]{1,0:T(8,128)} %get-tuple-element.133.refs_0_), custom_call_target="tpu_custom_call" | custom-call | flops 1000 | bytes 1000 | tf_op jit(solution)/shard_map/weight_gradient/pallas_call | solution.py:501
  264.2 8.1 %weight_gradient.5 = (bf16[2048,1536]{1,0:T(8,128)(2,1)}, f32[8,128]{1,0:T(8,128)}) custom-call(bf16[1152,2048]{1,0:T(8,128)(2,1)} %get-tuple-element.131.left_ref, bf16[1152,768]{1,0:T(8,128)(2,1)} %get-tuple-element.136.right_ref, f32[8,128]{1,0:T(8,128)} %get-tuple-element.137.refs_0_, ...), custom_call_target="tpu_custom_call", output_to_operand_aliasing={{0}: (3, {})} | custom-call | flops 1000 | bytes 1000 | tf_op jit(solution)/shard_map/weight_gradient/pallas_call | solution.py:501
  273.7 9.8 %collective-permute-done.24 = bf16[128,1024]{1,0:T(8,128)(2,1)S(1)} collective-permute-done((bf16[128,1024]{1,0:T(8,128)(2,1)S(1)}, bf16[128,1024]{1,0:T(8,128)(2,1)S(1)}, u32[]{:S(2)}, u32[]{:S(2)}) %collective-permute-start.24) | collective-permute-done | bytes 262176 | tf_op jit(solution)/shard_map/ppermute | solution.py:727
  290.7 2.4 collective-permute-start.27
  295.4 3.6 %collective-permute-start.30 = (bf16[1024,128]{1,0:T(8,128)(2,1)}, bf16[1024,128]{1,0:T(8,128)(2,1)}, u32[]{:S(2)}, u32[]{:S(2)}) collective-permute-start(bf16[1024,128]{1,0:T(8,128)(2,1)} %add_convert_fusion.4), channel_id=1, source_target_pairs={{0,0},{4,16},{8,4},{12,20},{16,8},{20,24},{24,12},{28,28},{1,1},{5... | collective-permute-start | bytes 786440 | tf_op jit(solution)/shard_map/ppermute | solution.py:805
  301.9 2.0 fusion.4
  303.8 1.7 copy.71
  (149 shorter events, 44.3 us)
Async XLA Ops:
  7.2 34.2 %copy-start = (bf16[1024,1024]{1,0:T(8,128)(2,1)S(1)}, bf16[1024,1024]{1,0:T(8,128)(2,1)}, u32[]{:S(2)}) copy-start(bf16[1024,1024]{1,0:T(8,128)(2,1)} %param.20) | copy-start | bytes 6291460
  7.2 60.0 %all-gather.7.cloned.1.call-start = ((), (), s32[]{:S(2)}) async-start(), calls=%async_computation.9 | async-start | bytes 2949120 | tf_op jit(solution)/shard_map/all_gather | solution.py:585
  9.3 2.4 collective-permute-start
  16.2 21.1 %all-to-all-start.1 = ((bf16[4,1,72,2048]{3,2,1,0:T(8,128)(2,1)}), bf16[4,1,72,2048]{3,2,1,0:T(8,128)(2,1)}, u32[]{:S(2)}, u32[]{:S(2)}) async-start(bf16[4,1,72,2048]{3,2,1,0:T(8,128)(2,1)} %get-tuple-element.78), calls=%async_computation.1 | async-start | bytes 2359296 | tf_op jit(solution)/shard_map/all_to_all | solution.py:594
  21.3 87.8 %all-gather.5.cloned.1.call-start = ((), (), s32[]{:S(2)}) async-start(), calls=%async_computation.8 | async-start | bytes 2621440 | tf_op jit(solution)/shard_map/all_gather | solution.py:586
  21.3 2.0 collective-permute-start.1
  24.1 16.8 %copy-start.27 = (s32[8]{0:T(128)S(1)}, s32[8]{0:T(128)}, u32[]{:S(2)}) copy-start(s32[8]{0:T(128)} %param.21) | copy-start | bytes 100
  24.1 16.8 %copy-start.25 = (bf16[128,512]{1,0:T(8,128)(2,1)S(1)}, bf16[128,512]{1,0:T(8,128)(2,1)}, u32[]{:S(2)}) copy-start(bf16[128,512]{1,0:T(8,128)(2,1)} %param.19) | copy-start | bytes 393220
  27.5 13.8 %copy-start.26 = (f32[4,128]{1,0:T(4,128)S(1)}, f32[4,128]{1,0:T(4,128)}, u32[]{:S(2)}) copy-start(f32[4,128]{1,0:T(4,128)} %param.23) | copy-start | bytes 6148
  37.4 18.6 %all-to-all-start = ((bf16[4,72,2048]{2,1,0:T(8,128)(2,1)}), bf16[4,72,2048]{2,1,0:T(8,128)(2,1)S(1)}, u32[]{:S(2)}, u32[]{:S(2)}) async-start(bf16[4,72,2048]{2,1,0:T(8,128)(2,1)} %select_scaled.4.refs_0_), calls=%async_computation | async-start | bytes 2359296 | tf_op jit(solution)/shard_map/all_to_all | solution.py:594
  67.2 4.9 %collective-permute-start.5 = (bf16[4,144,2048]{2,1,0:T(8,128)(2,1)}, bf16[4,144,2048]{2,1,0:T(8,128)(2,1)}, u32[]{:S(2)}, u32[]{:S(2)}) collective-permute-start(bf16[4,144,2048]{2,1,0:T(8,128)(2,1)} %bitcast.86), channel_id=1, source_target_pairs={{0,4},{4,0},{1,5},{5,1},{2,6},{6,2},{3,7},{7,3},{8,12},{12,8},{9,1... | collective-permute-start | bytes 7077896 | tf_op jit(solution)/shard_map/ppermute | solution.py:28
  67.3 12.6 %collective-permute-start.2 = (bf16[72,2048]{1,0:T(8,128)(2,1)}, bf16[72,2048]{1,0:T(8,128)(2,1)S(1)}, u32[]{:S(2)}, u32[]{:S(2)}) collective-permute-start(bf16[72,2048]{1,0:T(8,128)(2,1)} %get-tuple-element.82), channel_id=1, source_target_pairs={{0,1},{1,0},{2,3},{3,2},{4,5},{5,4},{6,7},{7,6},{8,9},{9,8},{10,11... | collective-permute-start | bytes 884744 | tf_op jit(solution)/shard_map/ppermute | solution.py:28
  68.8 15.6 %collective-permute-start.3 = (bf16[72,2048]{1,0:T(8,128)(2,1)}, bf16[72,2048]{1,0:T(8,128)(2,1)S(1)}, u32[]{:S(2)}, u32[]{:S(2)}) collective-permute-start(bf16[72,2048]{1,0:T(8,128)(2,1)} %get-tuple-element.83), channel_id=1, source_target_pairs={{0,2},{1,3},{2,0},{3,1},{4,6},{5,7},{6,4},{7,5},{8,10},{9,11},{10,... | collective-permute-start | bytes 884744 | tf_op jit(solution)/shard_map/ppermute | solution.py:28
  69.3 15.1 %collective-permute-start.4 = (bf16[72,2048]{1,0:T(8,128)(2,1)}, bf16[72,2048]{1,0:T(8,128)(2,1)S(1)}, u32[]{:S(2)}, u32[]{:S(2)}) collective-permute-start(bf16[72,2048]{1,0:T(8,128)(2,1)} %get-tuple-element.84), channel_id=1, source_target_pairs={{0,3},{1,2},{2,1},{3,0},{4,7},{5,6},{6,5},{7,4},{8,11},{9,10},{10,... | collective-permute-start | bytes 884744 | tf_op jit(solution)/shard_map/ppermute | solution.py:28
  85.2 45.0 %all-to-all-start.3 = ((bf16[4,3,72,2048]{3,2,1,0:T(8,128)(2,1)}), bf16[4,3,72,2048]{3,2,1,0:T(8,128)(2,1)}, u32[]{:S(2)}, u32[]{:S(2)}) async-start(bf16[4,3,72,2048]{3,2,1,0:T(8,128)(2,1)} %get-tuple-element.90), calls=%async_computation.3 | async-start | bytes 7077888 | tf_op jit(solution)/shard_map/all_to_all | solution.py:594
  109.2 4.4 %collective-permute-start.6 = (bf16[4,128,2048]{2,1,0:T(8,128)(2,1)}, bf16[4,128,2048]{2,1,0:T(8,128)(2,1)S(1)}, u32[]{:S(2)}, u32[]{:S(2)}) collective-permute-start(bf16[4,128,2048]{2,1,0:T(8,128)(2,1)} %bitcast.80), channel_id=1, source_target_pairs={{0,4},{4,0},{1,5},{5,1},{2,6},{6,2},{3,7},{7,3},{8,12},{12,8},{9,1... | collective-permute-start | bytes 6291464 | tf_op jit(solution)/shard_map/ppermute | solution.py:28
  130.2 18.0 %all-to-all-start.2 = ((bf16[4,72,2048]{2,1,0:T(8,128)(2,1)}), bf16[4,72,2048]{2,1,0:T(8,128)(2,1)S(1)}, u32[]{:S(2)}, u32[]{:S(2)}) async-start(bf16[4,72,2048]{2,1,0:T(8,128)(2,1)} %select_scaled.5.refs_0_), calls=%async_computation.2 | async-start | bytes 2359296 | tf_op jit(solution)/shard_map/all_to_all | solution.py:594
  149.3 18.0 %all-to-all-start.5 = ((bf16[4,72,2048]{2,1,0:T(8,128)(2,1)}), bf16[4,72,2048]{2,1,0:T(8,128)(2,1)S(1)}, u32[]{:S(2)}, u32[]{:S(2)}) async-start(bf16[4,72,2048]{2,1,0:T(8,128)(2,1)} %select_scaled.6.refs_4_), calls=%async_computation.5 | async-start | bytes 2359296 | tf_op jit(solution)/shard_map/all_to_all | solution.py:594
  168.3 29.8 %all-to-all-start.4 = ((bf16[4,72,2048]{2,1,0:T(8,128)(2,1)}), bf16[4,72,2048]{2,1,0:T(8,128)(2,1)S(1)}, u32[]{:S(2)}, u32[]{:S(2)}) async-start(bf16[4,72,2048]{2,1,0:T(8,128)(2,1)} %select_scaled.7.refs_4_), calls=%async_computation.4 | async-start | bytes 2359296 | tf_op jit(solution)/shard_map/all_to_all | solution.py:594
  171.8 130.0 %reduce-scatter.2.cloned.1.call-start = ((), (), s32[]{:S(2)}) async-start(), calls=%async_computation.7 | async-start | bytes 2621440 | tf_op jit(solution)/shard_map/reduce_scatter | solution.py:715
  185.0 10.3 %collective-permute-start.14 = (bf16[72,2048]{1,0:T(8,128)(2,1)}, bf16[72,2048]{1,0:T(8,128)(2,1)}, u32[]{:S(2)}, u32[]{:S(2)}) collective-permute-start(bf16[72,2048]{1,0:T(8,128)(2,1)} %get-tuple-element.117), channel_id=1, source_target_pairs={{0,1},{1,0},{2,3},{3,2},{4,5},{5,4},{6,7},{7,6},{8,9},{9,8},{10,11... | collective-permute-start | bytes 884744 | tf_op jit(solution)/shard_map/ppermute | solution.py:28
  187.0 22.2 %collective-permute-start.15 = (bf16[72,2048]{1,0:T(8,128)(2,1)}, bf16[72,2048]{1,0:T(8,128)(2,1)}, u32[]{:S(2)}, u32[]{:S(2)}) collective-permute-start(bf16[72,2048]{1,0:T(8,128)(2,1)} %get-tuple-element.118), channel_id=1, source_target_pairs={{0,2},{1,3},{2,0},{3,1},{4,6},{5,7},{6,4},{7,5},{8,10},{9,11},{10,... | collective-permute-start | bytes 884744 | tf_op jit(solution)/shard_map/ppermute | solution.py:28
  188.4 20.8 %collective-permute-start.16 = (bf16[72,2048]{1,0:T(8,128)(2,1)}, bf16[72,2048]{1,0:T(8,128)(2,1)}, u32[]{:S(2)}, u32[]{:S(2)}) collective-permute-start(bf16[72,2048]{1,0:T(8,128)(2,1)} %get-tuple-element.119), channel_id=1, source_target_pairs={{0,3},{1,2},{2,1},{3,0},{4,7},{5,6},{6,5},{7,4},{8,11},{9,10},{10,... | collective-permute-start | bytes 884744 | tf_op jit(solution)/shard_map/ppermute | solution.py:28
  188.5 26.0 %collective-permute-start.11 = (bf16[72,2048]{1,0:T(8,128)(2,1)}, bf16[72,2048]{1,0:T(8,128)(2,1)}, u32[]{:S(2)}, u32[]{:S(2)}) collective-permute-start(bf16[72,2048]{1,0:T(8,128)(2,1)} %get-tuple-element.114), channel_id=1, source_target_pairs={{0,1},{1,0},{2,3},{3,2},{4,5},{5,4},{6,7},{7,6},{8,9},{9,8},{10,11... | collective-permute-start | bytes 884744 | tf_op jit(solution)/shard_map/ppermute | solution.py:28
  190.4 29.5 %collective-permute-start.12 = (bf16[72,2048]{1,0:T(8,128)(2,1)}, bf16[72,2048]{1,0:T(8,128)(2,1)}, u32[]{:S(2)}, u32[]{:S(2)}) collective-permute-start(bf16[72,2048]{1,0:T(8,128)(2,1)} %get-tuple-element.115), channel_id=1, source_target_pairs={{0,2},{1,3},{2,0},{3,1},{4,6},{5,7},{6,4},{7,5},{8,10},{9,11},{10,... | collective-permute-start | bytes 884744 | tf_op jit(solution)/shard_map/ppermute | solution.py:28
  195.3 24.6 %collective-permute-start.13 = (bf16[72,2048]{1,0:T(8,128)(2,1)}, bf16[72,2048]{1,0:T(8,128)(2,1)}, u32[]{:S(2)}, u32[]{:S(2)}) collective-permute-start(bf16[72,2048]{1,0:T(8,128)(2,1)} %get-tuple-element.116), channel_id=1, source_target_pairs={{0,3},{1,2},{2,1},{3,0},{4,7},{5,6},{6,5},{7,4},{8,11},{9,10},{10,... | collective-permute-start | bytes 884744 | tf_op jit(solution)/shard_map/ppermute | solution.py:28
  209.1 16.3 %collective-permute-start.10 = (bf16[72,2048]{1,0:T(8,128)(2,1)}, bf16[72,2048]{1,0:T(8,128)(2,1)S(1)}, u32[]{:S(2)}, u32[]{:S(2)}) collective-permute-start(bf16[72,2048]{1,0:T(8,128)(2,1)} %get-tuple-element.113), channel_id=1, source_target_pairs={{0,3},{1,2},{2,1},{3,0},{4,7},{5,6},{6,5},{7,4},{8,11},{9,10},{10,... | collective-permute-start | bytes 884744 | tf_op jit(solution)/shard_map/ppermute | solution.py:28
  209.3 16.2 %collective-permute-start.8 = (bf16[72,2048]{1,0:T(8,128)(2,1)}, bf16[72,2048]{1,0:T(8,128)(2,1)S(1)}, u32[]{:S(2)}, u32[]{:S(2)}) collective-permute-start(bf16[72,2048]{1,0:T(8,128)(2,1)} %get-tuple-element.111), channel_id=1, source_target_pairs={{0,1},{1,0},{2,3},{3,2},{4,5},{5,4},{6,7},{7,6},{8,9},{9,8},{10,11... | collective-permute-start | bytes 884744 | tf_op jit(solution)/shard_map/ppermute | solution.py:28
  211.2 12.0 %copy-start.3 = (f32[128,2048]{1,0:T(8,128)S(1)}, f32[128,2048]{1,0:T(8,128)}, u32[]{:S(2)}) copy-start(f32[128,2048]{1,0:T(8,128)} %get-tuple-element.99.refs_4_) | copy-start | bytes 3145732
  211.2 12.0 %copy-start.6 = (bf16[128,2048]{1,0:T(8,128)(2,1)S(1)}, bf16[128,2048]{1,0:T(8,128)(2,1)}, u32[]{:S(2)}) copy-start(bf16[128,2048]{1,0:T(8,128)(2,1)} %param.13) | copy-start | bytes 1572868
  214.5 11.6 %collective-permute-start.9 = (bf16[72,2048]{1,0:T(8,128)(2,1)}, bf16[72,2048]{1,0:T(8,128)(2,1)S(1)}, u32[]{:S(2)}, u32[]{:S(2)}) collective-permute-start(bf16[72,2048]{1,0:T(8,128)(2,1)} %get-tuple-element.112), channel_id=1, source_target_pairs={{0,2},{1,3},{2,0},{3,1},{4,6},{5,7},{6,4},{7,5},{8,10},{9,11},{10,... | collective-permute-start | bytes 884744 | tf_op jit(solution)/shard_map/ppermute | solution.py:28
  224.8 5.8 %collective-permute-start.20 = (bf16[128,1024]{1,0:T(8,128)(2,1)S(1)}, bf16[128,1024]{1,0:T(8,128)(2,1)S(1)}, u32[]{:S(2)}, u32[]{:S(2)}) collective-permute-start(bf16[128,1024]{1,0:T(8,128)(2,1)S(1)} %select_convert_fusion.1), channel_id=1, source_target_pairs={{0,4},{4,0},{1,5},{5,1},{2,6},{6,2},{3,7},{7,3},{8,12},{12,8},{9,1... | collective-permute-start | bytes 786440 | tf_op jit(solution)/shard_map/ppermute | solution.py:28
  224.9 18.5 %collective-permute-start.7 = (bf16[128,2048]{1,0:T(8,128)(2,1)}, bf16[128,2048]{1,0:T(8,128)(2,1)}, u32[]{:S(2)}, u32[]{:S(2)}) collective-permute-start(bf16[128,2048]{1,0:T(8,128)(2,1)} %get-tuple-element.100), channel_id=1, source_target_pairs={{0,4},{4,0},{1,5},{5,1},{2,6},{6,2},{3,7},{7,3},{8,12},{12,8},{9,1... | collective-permute-start | bytes 1572872 | tf_op jit(solution)/shard_map/ppermute | solution.py:28
  225.4 18.0 %collective-permute-start.19 = (bf16[128,2048]{1,0:T(8,128)(2,1)}, bf16[128,2048]{1,0:T(8,128)(2,1)S(1)}, u32[]{:S(2)}, u32[]{:S(2)}) collective-permute-start(bf16[128,2048]{1,0:T(8,128)(2,1)} %get-tuple-element.125), channel_id=1, source_target_pairs={{0,4},{4,0},{1,5},{5,1},{2,6},{6,2},{3,7},{7,3},{8,12},{12,8},{9,1... | collective-permute-start | bytes 1572872 | tf_op jit(solution)/shard_map/ppermute | solution.py:28
  225.5 17.9 %collective-permute-start.18 = (bf16[128,2048]{1,0:T(8,128)(2,1)}, bf16[128,2048]{1,0:T(8,128)(2,1)}, u32[]{:S(2)}, u32[]{:S(2)}) collective-permute-start(bf16[128,2048]{1,0:T(8,128)(2,1)} %get-tuple-element.124), channel_id=1, source_target_pairs={{0,4},{4,0},{1,5},{5,1},{2,6},{6,2},{3,7},{7,3},{8,12},{12,8},{9,1... | collective-permute-start | bytes 1572872 | tf_op jit(solution)/shard_map/ppermute | solution.py:28
  230.2 13.2 %collective-permute-start.17 = (bf16[128,2048]{1,0:T(8,128)(2,1)}, bf16[128,2048]{1,0:T(8,128)(2,1)}, u32[]{:S(2)}, u32[]{:S(2)}) collective-permute-start(bf16[128,2048]{1,0:T(8,128)(2,1)} %get-tuple-element.123), channel_id=1, source_target_pairs={{0,4},{4,0},{1,5},{5,1},{2,6},{6,2},{3,7},{7,3},{8,12},{12,8},{9,1... | collective-permute-start | bytes 1572872 | tf_op jit(solution)/shard_map/ppermute | solution.py:28
  230.7 9.9 %collective-permute-start.21 = (bf16[128,1024]{1,0:T(8,128)(2,1)S(1)}, bf16[128,1024]{1,0:T(8,128)(2,1)S(1)}, u32[]{:S(2)}, u32[]{:S(2)}) collective-permute-start(bf16[128,1024]{1,0:T(8,128)(2,1)S(1)} %add_convert_fusion.7), channel_id=1, source_target_pairs={{0,8},{8,0},{16,24},{24,16},{1,9},{9,1},{17,25},{25,17},{2,10},{10... | collective-permute-start | bytes 786440 | tf_op jit(solution)/shard_map/ppermute | solution.py:28
  232.3 11.2 %copy-start.12 = (f32[128,2048]{1,0:T(8,128)S(1)}, f32[128,2048]{1,0:T(8,128)}, u32[]{:S(2)}) copy-start(f32[128,2048]{1,0:T(8,128)} %get-tuple-element.120.refs_4_) | copy-start | bytes 3145732
  240.7 14.6 %collective-permute-start.22 = (bf16[128,1024]{1,0:T(8,128)(2,1)S(1)}, bf16[128,1024]{1,0:T(8,128)(2,1)S(1)}, u32[]{:S(2)}, u32[]{:S(2)}) collective-permute-start(bf16[128,1024]{1,0:T(8,128)(2,1)S(1)} %add_convert_fusion.6), channel_id=1, source_target_pairs={{0,16},{8,24},{16,0},{24,8},{1,17},{9,25},{17,1},{25,9},{2,18},{10... | collective-permute-start | bytes 786440 | tf_op jit(solution)/shard_map/ppermute | solution.py:28
  263.5 8.8 %collective-permute-start.23 = (bf16[128,1024]{1,0:T(8,128)(2,1)S(1)}, bf16[128,1024]{1,0:T(8,128)(2,1)S(1)}, u32[]{:S(2)}, u32[]{:S(2)}) collective-permute-start(bf16[128,1024]{1,0:T(8,128)(2,1)S(1)} %fusion.7), channel_id=1, source_target_pairs={{3,2},{7,6},{11,10},{15,14},{19,18},{23,22},{27,26},{31,30}} | collective-permute-start | bytes 786440 | tf_op jit(solution)/shard_map/ppermute | solution.py:727
  264.2 19.5 %copy-start.15 = (bf16[128,512]{1,0:T(8,128)(2,1)S(1)}, bf16[128,512]{1,0:T(8,128)(2,1)}, u32[]{:S(2)}) copy-start(bf16[128,512]{1,0:T(8,128)(2,1)} %param.22) | copy-start | bytes 393220
  272.4 11.1 %collective-permute-start.24 = (bf16[128,1024]{1,0:T(8,128)(2,1)S(1)}, bf16[128,1024]{1,0:T(8,128)(2,1)S(1)}, u32[]{:S(2)}, u32[]{:S(2)}) collective-permute-start(bf16[128,1024]{1,0:T(8,128)(2,1)S(1)} %add.134), channel_id=1, source_target_pairs={{3,1},{2,0},{7,5},{6,4},{11,9},{10,8},{15,13},{14,12},{19,17},{18,... | collective-permute-start | bytes 786440 | tf_op jit(solution)/shard_map/ppermute | solution.py:727
  283.6 1.7 collective-permute-start.25
  289.3 5.3 %collective-permute-start.26 = (bf16[1024,128]{1,0:T(8,128)(2,1)S(1)}, bf16[1024,128]{1,0:T(8,128)(2,1)S(1)}, u32[]{:S(2)}, u32[]{:S(2)}) collective-permute-start(bf16[1024,128]{1,0:T(8,128)(2,1)S(1)} %get-tuple-element.176), channel_id=1, source_target_pairs={{0,4},{4,0},{1,5},{5,1},{2,6},{6,2},{3,7},{7,3},{8,12},{12,8},{9,1... | collective-permute-start | bytes 786440 | tf_op jit(solution)/shard_map/ppermute | solution.py:28
  290.7 9.6 %collective-permute-start.27 = (f32[32,512]{1,0:T(8,128)}, f32[32,512]{1,0:T(8,128)}, u32[]{:S(2)}, u32[]{:S(2)}) collective-permute-start(f32[32,512]{1,0:T(8,128)} %get-tuple-element.173), channel_id=1, source_target_pairs={{0,1},{1,0},{2,3},{3,2},{4,5},{5,4},{6,7},{7,6},{8,9},{9,8},{10,11... | collective-permute-start | bytes 196616 | tf_op jit(solution)/shard_map/ppermute | solution.py:28
  293.1 7.2 %collective-permute-start.28 = (f32[32,512]{1,0:T(8,128)}, f32[32,512]{1,0:T(8,128)}, u32[]{:S(2)}, u32[]{:S(2)}) collective-permute-start(f32[32,512]{1,0:T(8,128)} %get-tuple-element.175), channel_id=1, source_target_pairs={{0,2},{1,3},{2,0},{3,1},{4,6},{5,7},{6,4},{7,5},{8,10},{9,11},{10,... | collective-permute-start | bytes 196616 | tf_op jit(solution)/shard_map/ppermute | solution.py:28
  293.1 7.2 %collective-permute-start.29 = (f32[32,512]{1,0:T(8,128)}, f32[32,512]{1,0:T(8,128)}, u32[]{:S(2)}, u32[]{:S(2)}) collective-permute-start(f32[32,512]{1,0:T(8,128)} %get-tuple-element.174), channel_id=1, source_target_pairs={{0,3},{1,2},{2,1},{3,0},{4,7},{5,6},{6,5},{7,4},{8,11},{9,10},{10,... | collective-permute-start | bytes 196616 | tf_op jit(solution)/shard_map/ppermute | solution.py:28
  295.4 6.5 %collective-permute-start.30 = (bf16[1024,128]{1,0:T(8,128)(2,1)}, bf16[1024,128]{1,0:T(8,128)(2,1)}, u32[]{:S(2)}, u32[]{:S(2)}) collective-permute-start(bf16[1024,128]{1,0:T(8,128)(2,1)} %add_convert_fusion.4), channel_id=1, source_target_pairs={{0,0},{4,16},{8,4},{12,20},{16,8},{20,24},{24,12},{28,28},{1,1},{5... | collective-permute-start | bytes 786440 | tf_op jit(solution)/shard_map/ppermute | solution.py:805
  (20 other events, 59.5 us)
Sparse Core Ops, SparseCore 0:
  9.6 53.1 all-gather.6
  64.4 44.7 all-gather.4
  255.4 44.0 reduce-scatter.1
